TPU v7x, 128 devices: a whole 4x4x4 slice. The times are simulated.
128 devices in a mesh: dom: 64 (over x_hi, y, z, core), band: 2 (over x_lo).
Axes of the slice: x: 4 (x_hi: 2, x_lo: 2; x = x_hi * 2 + x_lo), y: 4, z: 4, core: 2. Of those that a mesh axis runs over, the one named last changes fastest.
Arguments:
- states: bfloat16 [1051392, 256], P('dom', 'band'), may hold values from -6 to 6
- mass_scale: float32 [1051392], P('dom'), may hold values from 0.5 to 2
- potential: float32 [64, 36864], P(None, 'dom'), may hold values from -6 to 6
- kinetic: bfloat16 [64, 64], replicated, may hold values from -0.75 to 0.75
- basis_fn: bfloat16 [64, 64], replicated, may hold values from -0.75 to 0.75
- connectivity: int32 [64, 36864], P(None, 'dom'), may hold values from 0 to 17796, as said below
- boundary: int32 [87616], P('dom'), may hold values from 0 to 16427, as said below
- owners: int32 [8, 8], replicated, may hold values from 0 to 63, as said below
Outputs:
- filtered: bfloat16 [1051392, 256], P('dom', 'band')
- projected: float32 [256, 2, 2, 1024], P('dom', 'band')
Inputs may be any that keep to these rules, and one draw needn't show every extreme that they name: `connectivity`: entries below 16428 are distinct owned nodes of the cell's domain; the others name the plane of the domain above. `boundary`: each domain's 1369 entries are distinct local node numbers. `owners`: in every column block of tiles no domain owns more than 4 tiles, and some domain owns exactly 4.
All inputs are finite; a program needn't handle non-finite values.
Results may differ from a plain program's by a relative error of at most 0.015.
Values may be sent and summed in bfloat16 or wider, within the bound.
No kernel may reach another device: no remote copies, remote signals or barrier semaphores. Data moves between devices by JAX's collectives and lax.ppermute only.
A program may use at most 128 MiB of HBM per device.

v0:
```python
import jax
import jax.numpy as jnp
from jax import lax
from jax.sharding import PartitionSpec as P

NPC = 64
QP = 64
TILE = 32
CAP = 4
CY = 12
CZ = 12


CENTER = 1.0
INV_HALF = 0.25
EXACT = lax.Precision.HIGHEST


def from_behind(value, axis, steps):
    count = lax.axis_size(axis)
    initial, last = (max(0, -steps), min(count, count - steps))
    return lax.ppermute(value, axis, [(source, source + steps) for source in range(initial, last)])


def local(states, mass_scale, potential, kinetic, basis_fn, connectivity, boundary, owners):
    node_count, state_count = states.shape
    plane_count = boundary.shape[0]
    cell_count = connectivity.shape[1]
    layer_cells = CY * CZ
    rounds = cell_count // layer_cells
    mass_col = mass_scale[:, None]

    def layer_work(source, layer, totals):
        cell_nodes = lax.dynamic_slice_in_dim(connectivity, layer * layer_cells, layer_cells, 1)
        quad_pot = lax.dynamic_slice_in_dim(potential, layer * layer_cells, layer_cells, 1)
        cell_vals = source[cell_nodes].reshape(NPC, layer_cells * state_count)
        at_points = jnp.dot(basis_fn, cell_vals, preferred_element_type=jnp.float32)
        at_points = at_points.reshape(QP, layer_cells, state_count)
        weighted = (
            (quad_pot[:, :, None] * at_points)
            .astype(jnp.bfloat16)
            .reshape(QP, layer_cells * state_count)
        )
        result = jnp.dot(basis_fn.T, weighted, preferred_element_type=jnp.float32)
        result = result + jnp.dot(kinetic, cell_vals, preferred_element_type=jnp.float32)
        return totals.at[cell_nodes].add(result.reshape(NPC, layer_cells, state_count))

    def operate(values):
        scaled = (mass_col * values.astype(jnp.float32)).astype(jnp.bfloat16)
        totals = jnp.zeros((node_count + plane_count, state_count), jnp.float32)
        ghost_vals = from_behind(scaled[boundary], "dom", -1)
        extended = jnp.concatenate([scaled, ghost_vals], 0)
        totals = lax.fori_loop(0, rounds, lambda step, acc: layer_work(extended, step, acc), totals)
        outgoing = totals[node_count:].astype(jnp.bfloat16)
        incoming = from_behind(outgoing, "dom", 1)
        owned = totals[:node_count].at[boundary].add(incoming.astype(jnp.float32))
        return mass_col * owned

    start_vals = states.astype(jnp.float32)
    filtered_one = ((operate(states) - CENTER * start_vals) * INV_HALF).astype(jnp.bfloat16)
    second = (
        2.0 * INV_HALF * (operate(filtered_one) - CENTER * filtered_one.astype(jnp.float32))
        - start_vals
    ).astype(jnp.bfloat16)
    image_vals = operate(second).astype(jnp.bfloat16)
    inverse = 1.0 / (node_count * lax.axis_size("dom"))
    shard_cols = lax.all_gather(second, "band", axis=1, tiled=True)
    ham_part = jnp.einsum("ns,nt->st", shard_cols, image_vals, preferred_element_type=jnp.float32)
    intersection_part = jnp.einsum(
        "ns,nt->st", shard_cols, second, preferred_element_type=jnp.float32
    )
    pair_mats = jnp.stack([ham_part, intersection_part]) * inverse
    total_rows = pair_mats.shape[1]
    tile_rows = total_rows // TILE
    tile_cols = state_count // TILE
    tile_count = tile_rows * tile_cols
    tile_vals = (
        pair_mats.reshape(2, tile_rows, TILE, tile_cols, TILE)
        .transpose(1, 3, 0, 2, 4)
        .reshape(tile_count, 2, TILE * TILE)
    )
    holder = lax.dynamic_slice_in_dim(
        owners, lax.axis_index("band") * tile_cols, tile_cols, 1
    ).reshape(tile_count)
    spots = jnp.arange(tile_count, dtype=jnp.int32)
    earlier = (holder[:, None] == holder[None, :]) & (spots[None, :] < spots[:, None])
    order_rank = jnp.sum(earlier.astype(jnp.int32), axis=1)
    slots = jnp.arange(CAP, dtype=jnp.int32)
    domains = jnp.arange(lax.axis_size("dom"), dtype=jnp.int32)
    chosen = (holder[None, None, :] == domains[:, None, None]) & (
        order_rank[None, None, :] == slots[None, :, None]
    )
    buffer = jnp.einsum("dct,tkx->dckx", chosen.astype(jnp.float32), tile_vals, precision=EXACT)
    buffer = buffer.reshape(lax.axis_size("dom") * CAP, 2, TILE * TILE)
    mine = lax.psum_scatter(buffer, "dom", scatter_dimension=0, tiled=True)
    return (second, mine[:, None])


def solution(mesh):
    return jax.shard_map(
        local,
        mesh=mesh,
        in_specs=(
            P("dom", "band"),
            P("dom"),
            P(None, "dom"),
            P(),
            P(),
            P(None, "dom"),
            P("dom"),
            P(),
        ),
        out_specs=(P("dom", "band"), P("dom", "band", None, None)),
        check_vma=False,
    )
```

profile of v0, /device:TPU:0, one launch (start us, length us, event | category | flops | bytes accessed | tf_op | source)
XLA Modules:
  0.0 2233.2 jit_solution(11111279634989481251)
XLA Ops:
  8.5 8.2 fusion.14
  25.8 12.7 pad_maximum_fusion
  42.3 443.6 %while.39 = (s32[]{:T(128)}, f32[17797,128]{1,0:T(8,128)}, s32[64,576]{1,0:T(8,128)S(1)}, f32[64,576]{1,0:T(8,128)S(1)}, bf16[17797,128]{1,0:T(8,128)(2,1)}, /*i...) while((s32[]{:T(128)}, f32[17797,128]{1,0:T(8,128)}, ...), condition=%wide.region_2.0_spmd, body=%wide.region_0.0_spmd.sunk | while | flops 457740288 | bytes 61763744 | solution.py:53
  42.5 34.5 %gather_fusion = bf16[9216,128]{1,0:T(8,128)(2,1)} fusion(bf16[17797,128]{1,0:T(8,128)(2,1)} %get-tuple-element.584, s32[9216]{0:T(1024)S(1)} %broadcast_clamp_fusion.6), kind=kCustom, calls=%fused_computation.clone.1 | custom fusion | bytes 4755456 | tf_op jit(solution)/shard_map/while/body/eval_jaxpr/gather | solution.py:36
  101.4 51.8 %scatter_fusion = f32[17797,128]{1,0:T(8,128)} fusion(f32[17797,128]{1,0:T(8,128)} %get-tuple-element.570, s32[9216]{0:T(1024)S(1)} %reshape.306, f32[9216,128]{1,0:T(8,128)} %reshape.308), kind=kCustom, calls=%fused_computation.6.clone.1 | custom fusion | flops 1179648 | bytes 14192640 | tf_op jit(solution)/shard_map/while/body/eval_jaxpr/scatter-add | solution.py:46
  153.4 34.5 %gather_fusion = bf16[9216,128]{1,0:T(8,128)(2,1)} fusion(bf16[17797,128]{1,0:T(8,128)(2,1)} %get-tuple-element.584, s32[9216]{0:T(1024)S(1)} %broadcast_clamp_fusion.6), kind=kCustom, calls=%fused_computation.clone.1 | custom fusion | bytes 4755456 | tf_op jit(solution)/shard_map/while/body/eval_jaxpr/gather | solution.py:36
  212.3 51.8 %scatter_fusion = f32[17797,128]{1,0:T(8,128)} fusion(f32[17797,128]{1,0:T(8,128)} %get-tuple-element.570, s32[9216]{0:T(1024)S(1)} %reshape.306, f32[9216,128]{1,0:T(8,128)} %reshape.308), kind=kCustom, calls=%fused_computation.6.clone.1 | custom fusion | flops 1179648 | bytes 14192640 | tf_op jit(solution)/shard_map/while/body/eval_jaxpr/scatter-add | solution.py:46
  264.3 34.5 %gather_fusion = bf16[9216,128]{1,0:T(8,128)(2,1)} fusion(bf16[17797,128]{1,0:T(8,128)(2,1)} %get-tuple-element.584, s32[9216]{0:T(1024)S(1)} %broadcast_clamp_fusion.6), kind=kCustom, calls=%fused_computation.clone.1 | custom fusion | bytes 4755456 | tf_op jit(solution)/shard_map/while/body/eval_jaxpr/gather | solution.py:36
  323.2 51.8 %scatter_fusion = f32[17797,128]{1,0:T(8,128)} fusion(f32[17797,128]{1,0:T(8,128)} %get-tuple-element.570, s32[9216]{0:T(1024)S(1)} %reshape.306, f32[9216,128]{1,0:T(8,128)} %reshape.308), kind=kCustom, calls=%fused_computation.6.clone.1 | custom fusion | flops 1179648 | bytes 14192640 | tf_op jit(solution)/shard_map/while/body/eval_jaxpr/scatter-add | solution.py:46
  375.2 34.5 %gather_fusion = bf16[9216,128]{1,0:T(8,128)(2,1)} fusion(bf16[17797,128]{1,0:T(8,128)(2,1)} %get-tuple-element.584, s32[9216]{0:T(1024)S(1)} %broadcast_clamp_fusion.6), kind=kCustom, calls=%fused_computation.clone.1 | custom fusion | bytes 4755456 | tf_op jit(solution)/shard_map/while/body/eval_jaxpr/gather | solution.py:36
  434.1 51.8 %scatter_fusion = f32[17797,128]{1,0:T(8,128)} fusion(f32[17797,128]{1,0:T(8,128)} %get-tuple-element.570, s32[9216]{0:T(1024)S(1)} %reshape.306, f32[9216,128]{1,0:T(8,128)} %reshape.308), kind=kCustom, calls=%fused_computation.6.clone.1 | custom fusion | flops 1179648 | bytes 14192640 | tf_op jit(solution)/shard_map/while/body/eval_jaxpr/scatter-add | solution.py:46
  487.1 7.8 collective-permute-start.1
  494.9 7.7 slice.21
  502.6 15.8 scatter_custom_fusion.3
  518.3 10.5 fusion.12
  537.9 12.7 pad_maximum_fusion.1
  554.4 443.3 %while.40 = (s32[]{:T(128)}, f32[17797,128]{1,0:T(8,128)}, s32[64,576]{1,0:T(8,128)S(1)}, f32[64,576]{1,0:T(8,128)S(1)}, bf16[17797,128]{1,0:T(8,128)(2,1)}, /*i...) while((s32[]{:T(128)}, f32[17797,128]{1,0:T(8,128)}, ...), condition=%wide.region_6.0_spmd, body=%wide.region_4.0_spmd.sunk | while | flops 457740288 | bytes 61763744 | solution.py:53
  554.6 34.5 %gather_fusion.1 = bf16[9216,128]{1,0:T(8,128)(2,1)} fusion(bf16[17797,128]{1,0:T(8,128)(2,1)} %get-tuple-element.617, s32[9216]{0:T(1024)S(1)} %broadcast_clamp_fusion.7), kind=kCustom, calls=%fused_computation.1.clone.1 | custom fusion | bytes 4755456 | tf_op jit(solution)/shard_map/while/body/eval_jaxpr/gather | solution.py:36
  613.4 51.8 %scatter_fusion.1 = f32[17797,128]{1,0:T(8,128)} fusion(f32[17797,128]{1,0:T(8,128)} %get-tuple-element.603, s32[9216]{0:T(1024)S(1)} %reshape.313, f32[9216,128]{1,0:T(8,128)} %reshape.315), kind=kCustom, calls=%fused_computation.7.clone.1 | custom fusion | flops 1179648 | bytes 14192640 | tf_op jit(solution)/shard_map/while/body/eval_jaxpr/scatter-add | solution.py:46
  665.4 34.5 %gather_fusion.1 = bf16[9216,128]{1,0:T(8,128)(2,1)} fusion(bf16[17797,128]{1,0:T(8,128)(2,1)} %get-tuple-element.617, s32[9216]{0:T(1024)S(1)} %broadcast_clamp_fusion.7), kind=kCustom, calls=%fused_computation.1.clone.1 | custom fusion | bytes 4755456 | tf_op jit(solution)/shard_map/while/body/eval_jaxpr/gather | solution.py:36
  724.2 51.8 %scatter_fusion.1 = f32[17797,128]{1,0:T(8,128)} fusion(f32[17797,128]{1,0:T(8,128)} %get-tuple-element.603, s32[9216]{0:T(1024)S(1)} %reshape.313, f32[9216,128]{1,0:T(8,128)} %reshape.315), kind=kCustom, calls=%fused_computation.7.clone.1 | custom fusion | flops 1179648 | bytes 14192640 | tf_op jit(solution)/shard_map/while/body/eval_jaxpr/scatter-add | solution.py:46
  776.2 34.5 %gather_fusion.1 = bf16[9216,128]{1,0:T(8,128)(2,1)} fusion(bf16[17797,128]{1,0:T(8,128)(2,1)} %get-tuple-element.617, s32[9216]{0:T(1024)S(1)} %broadcast_clamp_fusion.7), kind=kCustom, calls=%fused_computation.1.clone.1 | custom fusion | bytes 4755456 | tf_op jit(solution)/shard_map/while/body/eval_jaxpr/gather | solution.py:36
  835.1 51.8 %scatter_fusion.1 = f32[17797,128]{1,0:T(8,128)} fusion(f32[17797,128]{1,0:T(8,128)} %get-tuple-element.603, s32[9216]{0:T(1024)S(1)} %reshape.313, f32[9216,128]{1,0:T(8,128)} %reshape.315), kind=kCustom, calls=%fused_computation.7.clone.1 | custom fusion | flops 1179648 | bytes 14192640 | tf_op jit(solution)/shard_map/while/body/eval_jaxpr/scatter-add | solution.py:46
  887.1 34.5 %gather_fusion.1 = bf16[9216,128]{1,0:T(8,128)(2,1)} fusion(bf16[17797,128]{1,0:T(8,128)(2,1)} %get-tuple-element.617, s32[9216]{0:T(1024)S(1)} %broadcast_clamp_fusion.7), kind=kCustom, calls=%fused_computation.1.clone.1 | custom fusion | bytes 4755456 | tf_op jit(solution)/shard_map/while/body/eval_jaxpr/gather | solution.py:36
  927.9 7.3 fusion.84
  945.9 51.8 %scatter_fusion.1 = f32[17797,128]{1,0:T(8,128)} fusion(f32[17797,128]{1,0:T(8,128)} %get-tuple-element.603, s32[9216]{0:T(1024)S(1)} %reshape.313, f32[9216,128]{1,0:T(8,128)} %reshape.315), kind=kCustom, calls=%fused_computation.7.clone.1 | custom fusion | flops 1179648 | bytes 14192640 | tf_op jit(solution)/shard_map/while/body/eval_jaxpr/scatter-add | solution.py:46
  998.9 7.5 collective-permute-start.3
  1006.4 7.8 slice.23
  1014.1 15.8 scatter_custom_fusion.4
  1029.9 14.2 multiply_convert_fusion.1
  1053.2 12.7 pad_maximum_fusion.2
  1069.7 443.1 %while.41 = (s32[]{:T(128)}, f32[17797,128]{1,0:T(8,128)}, s32[64,576]{1,0:T(8,128)S(1)}, f32[64,576]{1,0:T(8,128)S(1)}, bf16[17797,128]{1,0:T(8,128)(2,1)}, /*i...) while((s32[]{:T(128)}, f32[17797,128]{1,0:T(8,128)}, ...), condition=%wide.region_11.0_spmd, body=%wide.region_9.11_spmd.sunk | while | flops 457740288 | bytes 61763744 | solution.py:53
  1069.9 34.4 %gather_fusion.2 = bf16[9216,128]{1,0:T(8,128)(2,1)} fusion(bf16[17797,128]{1,0:T(8,128)(2,1)} %get-tuple-element.650, s32[9216]{0:T(1024)S(1)} %broadcast_clamp_fusion.8), kind=kCustom, calls=%fused_computation.2.clone.1 | custom fusion | bytes 4755456 | tf_op jit(solution)/shard_map/while/body/eval_jaxpr/gather | solution.py:36
  1128.6 51.8 %scatter_fusion.2 = f32[17797,128]{1,0:T(8,128)} fusion(f32[17797,128]{1,0:T(8,128)} %get-tuple-element.636, s32[9216]{0:T(1024)S(1)} %reshape.320, f32[9216,128]{1,0:T(8,128)} %reshape.322), kind=kCustom, calls=%fused_computation.8.clone.1 | custom fusion | flops 1179648 | bytes 14192640 | tf_op jit(solution)/shard_map/while/body/eval_jaxpr/scatter-add | solution.py:46
  1180.7 34.4 %gather_fusion.2 = bf16[9216,128]{1,0:T(8,128)(2,1)} fusion(bf16[17797,128]{1,0:T(8,128)(2,1)} %get-tuple-element.650, s32[9216]{0:T(1024)S(1)} %broadcast_clamp_fusion.8), kind=kCustom, calls=%fused_computation.2.clone.1 | custom fusion | bytes 4755456 | tf_op jit(solution)/shard_map/while/body/eval_jaxpr/gather | solution.py:36
  1221.4 7.3 fusion.91
  1239.4 51.8 %scatter_fusion.2 = f32[17797,128]{1,0:T(8,128)} fusion(f32[17797,128]{1,0:T(8,128)} %get-tuple-element.636, s32[9216]{0:T(1024)S(1)} %reshape.320, f32[9216,128]{1,0:T(8,128)} %reshape.322), kind=kCustom, calls=%fused_computation.8.clone.1 | custom fusion | flops 1179648 | bytes 14192640 | tf_op jit(solution)/shard_map/while/body/eval_jaxpr/scatter-add | solution.py:46
  1291.4 34.4 %gather_fusion.2 = bf16[9216,128]{1,0:T(8,128)(2,1)} fusion(bf16[17797,128]{1,0:T(8,128)(2,1)} %get-tuple-element.650, s32[9216]{0:T(1024)S(1)} %broadcast_clamp_fusion.8), kind=kCustom, calls=%fused_computation.2.clone.1 | custom fusion | bytes 4755456 | tf_op jit(solution)/shard_map/while/body/eval_jaxpr/gather | solution.py:36
  1332.2 7.3 fusion.91
  1350.2 51.8 %scatter_fusion.2 = f32[17797,128]{1,0:T(8,128)} fusion(f32[17797,128]{1,0:T(8,128)} %get-tuple-element.636, s32[9216]{0:T(1024)S(1)} %reshape.320, f32[9216,128]{1,0:T(8,128)} %reshape.322), kind=kCustom, calls=%fused_computation.8.clone.1 | custom fusion | flops 1179648 | bytes 14192640 | tf_op jit(solution)/shard_map/while/body/eval_jaxpr/scatter-add | solution.py:46
  1402.2 34.4 %gather_fusion.2 = bf16[9216,128]{1,0:T(8,128)(2,1)} fusion(bf16[17797,128]{1,0:T(8,128)(2,1)} %get-tuple-element.650, s32[9216]{0:T(1024)S(1)} %broadcast_clamp_fusion.8), kind=kCustom, calls=%fused_computation.2.clone.1 | custom fusion | bytes 4755456 | tf_op jit(solution)/shard_map/while/body/eval_jaxpr/gather | solution.py:36
  1443.0 7.3 fusion.91
  1461.0 51.8 %scatter_fusion.2 = f32[17797,128]{1,0:T(8,128)} fusion(f32[17797,128]{1,0:T(8,128)} %get-tuple-element.636, s32[9216]{0:T(1024)S(1)} %reshape.320, f32[9216,128]{1,0:T(8,128)} %reshape.322), kind=kCustom, calls=%fused_computation.8.clone.1 | custom fusion | flops 1179648 | bytes 14192640 | tf_op jit(solution)/shard_map/while/body/eval_jaxpr/scatter-add | solution.py:46
  1514.0 7.9 collective-permute-start.5
  1522.0 7.8 slice.25
  1529.8 15.8 scatter_custom_fusion.5
  1545.5 10.6 fusion.18
  1568.3 656.3 %all-reduce.3.cloned.1.call-done = f32[256,2,1024]{2,0,1:T(8,128)} async-done(((f32[256,2,1024]{2,0,1:T(8,128)}), f32[256,2,1024]{2,0,1:T(8,128)}) %all-reduce.3.cloned.1.call-update) | async-done | bytes 2097168
  (175 shorter events, 321.4 us)
Async XLA Ops:
  7.2 1043.8 %copy-start = (s32[8,8]{1,0:T(8,128)S(1)}, s32[8,8]{1,0:T(8,128)}, u32[]{:S(2)}) copy-start(s32[8,8]{1,0:T(8,128)} %param.21) | copy-start | bytes 772
  7.2 1538.4 %all-gather.2.cloned.1.call-start = ((), (), s32[]{:S(2)}) async-start(), calls=%async_computation | async-start | bytes 12619776 | tf_op jit(solution)/shard_map/all_gather | solution.py:67
  7.9 0.6 copy-start.11
  8.5 8.2 copy-start.8
  22.2 3.6 collective-permute-start
  38.5 3.7 copy-start.1
  38.5 3.7 copy-start.2
  38.5 3.7 copy-start.3
  38.5 3.7 copy-start.4
  487.1 15.5 collective-permute-start.1
  502.6 15.8 copy-start.5
  518.3 10.5 copy-start.9
  534.4 3.6 collective-permute-start.2
  998.9 15.3 collective-permute-start.3
  1014.1 15.8 copy-start.6
  1029.9 14.2 copy-start.10
  1049.7 3.6 collective-permute-start.4
  1052.5 1172.1 %all-reduce.3.cloned.1.call-start = ((), (), s32[]{:S(2)}) async-start(), calls=%async_computation.1 | async-start | bytes 4194304
  1069.7 452.3 %copy-start.14 = (s32[32]{0:T(128)S(1)}, s32[32]{0:T(128)}, u32[]{:S(2)}) copy-start(s32[32]{0:T(128)} %convert_reduce_fusion) | copy-start | bytes 388
  1069.7 452.3 %copy-start.12 = (pred[64,32]{1,0:T(8,128)(4,1)S(1)}, pred[64,32]{1,0:T(8,128)(4,1)}, u32[]{:S(2)}) copy-start(pred[64,32]{1,0:T(8,128)(4,1)} %iota_compare_fusion) | copy-start | bytes 6148
  1514.0 15.8 collective-permute-start.5
  1529.8 15.8 copy-start.7
  1563.7 3.3 copy-start.13
Sparse Core Ops, SparseCore 0:
  1052.6 123.4 all-gather.1
  1567.2 657.4 all-reduce.2
where the time goes:
time: 2240 us; the launch traced here: 2230 us
  other arithmetic  744 us (33%)
  waiting for transfers between devices  661 us (30%)
  local copies, waits for them, and re-layouts  613 us (27%)
  matrix products  172 us (8%)
  starting transfers between devices  27.4 us (1%)
    unnamed x3, waiting for transfers between devices  656 us
    scatter-add x12, other arithmetic, layer_work(): totals.at[cell_nodes].add(result.reshape(NPC, layer_cells, state_count))  622 us
    gather x12, local copies, waits for them, and re-layouts, layer_work(): cell_vals = source[cell_nodes].reshape(NPC, layer_cells * state_count)  413 us
    dot_general x12, matrix products, layer_work(): result = jnp.dot(basis_fn.T, weighted, preferred_element_type=jnp.float32)  87.9 us
    dot_general x12, matrix products, layer_work(): jnp.dot(kinetic, cell_vals, preferred_element_type=jnp.float32)  64.5 us
    reshape x12, local copies, waits for them, and re-layouts, layer_work(): result.reshape(NPC, layer_cells, state_count)  63.2 us
    scatter-add x3, other arithmetic, operate(): owned = totals[:node_count].at[boundary].add(incoming.astype(jnp.float32))  47.3 us
  transfers between devices with their start and end apart: 8, of which 4 were waited for; matrix products, arithmetic and copies ran while one was open for 22% of the time, Pallas kernels for 0%

commit v1 on v0

v1 whole, which is shorter than its diff:
```python
import functools

import jax
import jax.numpy as jnp
from jax import lax
from jax.experimental import pallas as pl
from jax.experimental.pallas import tpu as pltpu
from jax.sharding import PartitionSpec as P

NPC = 64
QP = 64
TILE = 32
CAP = 4
CENTER = 1.0
INV_HALF = 0.25
EXACT = lax.Precision.HIGHEST

LANES = 128
ROWS = 128
GROUP = 4
BATCH = 8
STRIDE = 1024
F32 = jnp.float32
BF16 = jnp.bfloat16
VMEM = pl.BlockSpec(memory_space=pltpu.VMEM)
SMEM = pl.BlockSpec(memory_space=pltpu.SMEM)
ANY = pl.BlockSpec(memory_space=pl.ANY)


def round_up(count, unit):
    return -(-count // unit) * unit


def from_behind(value, axis, steps):
    count = lax.axis_size(axis)
    initial, last = (max(0, -steps), min(count, count - steps))
    return lax.ppermute(value, axis, [(source, source + steps) for source in range(initial, last)])


def params():
    return pltpu.CompilerParams(vmem_limit_bytes=62 << 20)


def by_rows(count, work):
    def step(i, _):
        work(pl.ds(pl.multiple_of(i * ROWS, ROWS), ROWS))
        return 0

    lax.fori_loop(0, count // ROWS, step, 0)


def by_entries(count, work):
    unroll = max(u for u in range(1, 65) if count % u == 0)

    def step(i, _):
        for j in range(unroll):
            work(i * unroll + j)
        return 0

    lax.fori_loop(0, count // unroll, step, 0)


def gather(src, lists, cells, out):
    for k, cell in enumerate(cells):
        for j in range(NPC):
            out[k * NPC + j : k * NPC + j + 1, :] = src[pl.ds(lists[j][cell], 1), :]


def multiply(vals, pot, base, stacked, basis_t, out):
    chunk = pl.multiple_of((base // LANES) * LANES, LANES)
    shift = lax.rem(LANES - lax.rem(base, LANES), LANES)
    columns = pltpu.roll(pot[:, pl.ds(chunk, LANES)], shift, 1)
    for p in range(0, GROUP, 2):
        pair = jnp.concatenate(
            [vals[k * NPC : (k + 1) * NPC, :] for k in (p, p + 1)], axis=1
        ).astype(BF16)
        both = jnp.dot(stacked, pair, preferred_element_type=F32)
        weight = jnp.concatenate(
            [jnp.broadcast_to(columns[:, k : k + 1], (QP, LANES)) for k in (p, p + 1)], axis=1
        )
        weighted = (weight * both[:QP]).astype(BF16)
        result = jnp.dot(basis_t, weighted, preferred_element_type=F32) + both[QP:]
        for k in (p, p + 1):
            out[k * NPC : (k + 1) * NPC, :] = result[:, (k - p) * LANES : (k - p + 1) * LANES]


def scatter(res, lists, cells, sums, batch):
    for p in range(0, GROUP, 2):
        for start in range(0, NPC, batch):
            moved = []
            for k in (p, p + 1):
                for j in range(start, start + batch):
                    row = pl.ds(lists[j][cells[k]], 1)
                    total = sums[k - p][row, :] + res[k * NPC + j : k * NPC + j + 1, :]
                    moved.append((k - p, row, total))
            for which, row, total in moved:
                sums[which][row, :] = total


def cells_of(group):
    return [group * GROUP + k for k in range(GROUP)]


def sweep(groups, src, lists, pot, stacked_ref, basis_t_ref, sums, vals, ress, repeated):
    stacked = stacked_ref[...]
    basis_t = basis_t_ref[...]

    def mult(slot, group):
        multiply(vals[slot], pot, group * GROUP, stacked, basis_t, ress[slot])

    def two(i, _):
        first = 2 * i
        gather(src, lists, cells_of(first + 1), vals[1])
        mult(0, first)
        scatter(ress[1], lists, cells_of(jnp.maximum(first - 1, 0)), sums, BATCH)
        gather(src, lists, cells_of(jnp.minimum(first + 2, groups - 1)), vals[0])
        mult(1, first + 1)
        scatter(ress[0], lists, cells_of(first), sums, BATCH)
        return 0

    @pl.when(repeated[0] == 0)
    def _():
        ress[1][...] = jnp.zeros_like(ress[1])
        gather(src, lists, cells_of(0), vals[0])
        lax.fori_loop(0, groups // 2, two, 0)
        scatter(ress[1], lists, cells_of(groups - 1), sums, BATCH)

    @pl.when(repeated[0] != 0)
    def _():
        def one(i, _):
            gather(src, lists, cells_of(i), vals[0])
            mult(0, i)
            scatter(ress[0], lists, cells_of(i), sums, 1)
            return 0

        lax.fori_loop(0, groups, one, 0)


def edge_kernel(edge_count, edge, states, mass, states_edge, mass_edge, wide):
    def widen(rows):
        wide[rows, :] = states[rows, :].astype(F32)

    by_rows(states.shape[0], widen)
    tail = states_edge.shape[0] - 8
    states_edge[tail:, :] = jnp.zeros((8, LANES), F32)
    mass_edge[tail:, :] = jnp.zeros((8, LANES), F32)

    def take(i):
        row = pl.ds(edge[i], 1)
        states_edge[pl.ds(i, 1), :] = wide[row, :]
        mass_edge[pl.ds(i, 1), :] = mass[row, :]

    by_entries(edge_count, take)


def apply_kernel(which, sizes, *refs):
    nodes, padded, edge_count, groups = sizes
    refs = list(refs)
    conn, edge, repeated, pot, stacked, basis_t, mass, values, ghost = refs[:9]
    del refs[:9]
    if which > 1:
        scaled_edge = refs.pop(0)
    if which == 2:
        states = refs.pop(0)
    if which == 3:
        second_edge = refs.pop(0)
    result, edge_sums, outgoing = refs[:3]
    del refs[:3]
    if which == 3:
        second = refs.pop(0)
    src, sum_a, sum_b, val_a, val_b, res_a, res_b, arrived = refs[:8]
    lists = refs[8:]
    copies = [
        pltpu.make_async_copy(conn.at[pl.ds(j * STRIDE, STRIDE)], lists[j], arrived.at[j])
        for j in range(NPC)
    ]
    for copy in copies:
        copy.start()
    ghost_count = ghost.shape[0]

    def prepare(rows):
        scaled = (mass[rows, :] * values[rows, :].astype(F32)).astype(BF16)
        src[rows, :] = scaled.astype(F32)

    by_rows(padded, prepare)
    src[padded : padded + ghost_count, :] = ghost[...].astype(F32)
    if which > 1:

        def patch(i):
            src[pl.ds(edge[i], 1), :] = scaled_edge[pl.ds(i, 1), :]

        by_entries(edge_count, patch)

    def clear(rows):
        sum_a[rows, :] = jnp.zeros((ROWS, LANES), F32)
        sum_b[rows, :] = jnp.zeros((ROWS, LANES), F32)

    by_rows(src.shape[0], clear)
    for copy in copies:
        copy.wait()

    sweep(
        groups,
        src,
        lists,
        pot,
        stacked,
        basis_t,
        (sum_a, sum_b),
        (val_a, val_b),
        (res_a, res_b),
        repeated,
    )

    ghost_rows = slice(padded, padded + ghost_count)
    outgoing[...] = (sum_a[ghost_rows, :] + sum_b[ghost_rows, :]).astype(BF16)
    tail = edge_sums.shape[0] - 8
    edge_sums[tail:, :] = jnp.zeros((8, LANES), F32)

    def take(i):
        row = pl.ds(edge[i], 1)
        edge_sums[pl.ds(i, 1), :] = sum_a[row, :] + sum_b[row, :]
        if which == 3:
            sum_a[row, :] = jnp.zeros((1, LANES), F32)
            sum_b[row, :] = jnp.zeros((1, LANES), F32)

    by_entries(edge_count, take)

    def finish(rows):
        image = mass[rows, :] * (sum_a[rows, :] + sum_b[rows, :])
        if which == 1:
            result[rows, :] = ((image - CENTER * values[rows, :].astype(F32)) * INV_HALF).astype(BF16)
        elif which == 2:
            result[rows, :] = (
                2.0 * INV_HALF * (image - CENTER * values[rows, :].astype(F32))
                - states[rows, :].astype(F32)
            ).astype(BF16)
        else:
            result[rows, :LANES] = image.astype(BF16)
            src[rows, :] = values[rows, :].astype(F32)

    by_rows(padded, finish)
    if which == 3:

        def blank(i):
            src[pl.ds(edge[i], 1), :] = jnp.zeros((1, LANES), F32)

        def fill(i):
            src[pl.ds(edge[i], 1), :] = second_edge[pl.ds(i, 1), :]

        def blanked(rows):
            result[rows, LANES:] = src[rows, :].astype(BF16)

        def filled(rows):
            second[rows, :] = src[rows, :].astype(BF16)

        by_entries(edge_count, blank)
        by_rows(padded, blanked)
        by_entries(edge_count, fill)
        whole = nodes // ROWS * ROWS
        by_rows(whole, filled)
        second[whole:nodes, :] = src[whole:nodes, :].astype(BF16)


def local(states, mass_scale, potential, kinetic, basis_fn, connectivity, boundary, owners):
    node_count, state_count = states.shape
    edge_count = boundary.shape[0]
    cell_count = connectivity.shape[1]
    padded = round_up(node_count, ROWS)
    edge_rows = round_up(edge_count, 16)
    total_rows = round_up(padded + edge_rows, ROWS)

    is_ghost = connectivity >= node_count
    lists = jnp.where(is_ghost, connectivity + (padded - node_count), connectivity)
    lists = jnp.pad(lists, ((0, 0), (0, STRIDE - cell_count))).reshape(-1)
    batched = jnp.where(is_ghost, connectivity, -1).reshape(NPC // BATCH, BATCH, cell_count)
    same = (batched[:, :, None] == batched[:, None, :]) & (batched[:, :, None] >= 0)
    apart = ~jnp.eye(BATCH, dtype=bool)[None, :, :, None]
    repeated = jnp.any(same & apart).astype(jnp.int32).reshape(1)
    pot = jnp.pad(potential, ((0, 0), (0, round_up(cell_count, LANES) - cell_count)))
    mass = jnp.pad(
        jnp.broadcast_to(mass_scale[:, None], (node_count, LANES)),
        ((0, padded - node_count), (0, 0)),
    )
    states_padded = jnp.pad(states, ((0, padded - node_count), (0, 0)))
    stacked = jnp.concatenate([basis_fn, kinetic], 0)
    basis_t = basis_fn.T

    edge_shape = jax.ShapeDtypeStruct((edge_rows, LANES), F32)
    edge_half = jax.ShapeDtypeStruct((edge_rows, LANES), BF16)
    wide_half = jax.ShapeDtypeStruct((padded, LANES), BF16)
    both_half = jax.ShapeDtypeStruct((padded, 2 * LANES), BF16)
    states_edge, mass_edge = pl.pallas_call(
        functools.partial(edge_kernel, edge_count),
        out_shape=(edge_shape, edge_shape),
        in_specs=[SMEM, VMEM, VMEM],
        out_specs=(VMEM, VMEM),
        scratch_shapes=[pltpu.VMEM((padded, LANES), F32)],
        compiler_params=params(),
        name="edge_rows",
    )(boundary, states_padded, mass)

    work = pltpu.VMEM((total_rows, LANES), F32)
    block = pltpu.VMEM((GROUP * NPC, LANES), F32)

    def operate(which, values, ghost, extra, outs):
        sizes = (node_count, padded, edge_count, cell_count // GROUP)
        return pl.pallas_call(
            functools.partial(apply_kernel, which, sizes),
            out_shape=outs,
            in_specs=[ANY, SMEM, SMEM] + [VMEM] * (6 + len(extra)),
            out_specs=(VMEM,) * len(outs),
            scratch_shapes=[work, work, work, block, block, block, block]
            + [pltpu.SemaphoreType.DMA((NPC,))]
            + [pltpu.SMEM((STRIDE,), jnp.int32)] * NPC,
            compiler_params=params(),
            name=f"apply_{which}",
        )(lists, boundary, repeated, pot, stacked, basis_t, mass, values, ghost, *extra)

    def joined(edge_sums, outgoing):
        incoming = from_behind(outgoing, "dom", 1)
        return mass_edge * (edge_sums + incoming.astype(F32))

    def scaled(edge):
        return (mass_edge * edge).astype(BF16)

    sent = scaled(states_edge)
    ghost = from_behind(sent, "dom", -1)
    one, sums, outgoing = operate(1, states_padded, ghost, (), (wide_half, edge_shape, edge_half))
    one_edge = ((joined(sums, outgoing) - CENTER * states_edge) * INV_HALF).astype(BF16).astype(F32)

    sent = scaled(one_edge)
    ghost = from_behind(sent, "dom", -1)
    two, sums, outgoing = operate(
        2, one, ghost, (sent.astype(F32), states_padded), (wide_half, edge_shape, edge_half)
    )
    shard_cols = lax.all_gather(two, "band", axis=1, tiled=True)
    two_half = (
        2.0 * INV_HALF * (joined(sums, outgoing) - CENTER * one_edge) - states_edge
    ).astype(BF16)
    two_edge = two_half.astype(F32)

    sent = scaled(two_edge)
    ghost = from_behind(sent, "dom", -1)
    edge_cols = lax.all_gather(two_half, "band", axis=1, tiled=True)
    own, sums, outgoing, second = operate(
        3,
        two,
        ghost,
        (sent.astype(F32), two_edge),
        (both_half, edge_shape, edge_half, jax.ShapeDtypeStruct((node_count, LANES), BF16)),
    )
    image_edge = joined(sums, outgoing).astype(BF16)
    own_edge = jnp.concatenate([image_edge, two_half], 1)

    def project(columns, mine):
        return lax.dot_general(
            columns, mine, (((0,), (0,)), ((), ())), preferred_element_type=F32
        )

    pair = project(shard_cols, own) + project(edge_cols, own_edge)
    inverse = 1.0 / (node_count * lax.axis_size("dom"))
    pair = lax.psum(pair * inverse, "dom")

    tile_rows = pair.shape[0] // TILE
    tile_cols = state_count // TILE
    tile_count = tile_rows * tile_cols
    tile_vals = (
        pair.reshape(tile_rows, TILE, 2, tile_cols, TILE)
        .transpose(0, 3, 2, 1, 4)
        .reshape(tile_count, 2 * TILE * TILE)
    )
    holder = lax.dynamic_slice_in_dim(
        owners, lax.axis_index("band") * tile_cols, tile_cols, 1
    ).reshape(tile_count)
    spots = jnp.arange(tile_count, dtype=jnp.int32)
    earlier = (holder[:, None] == holder[None, :]) & (spots[None, :] < spots[:, None])
    order_rank = jnp.sum(earlier.astype(jnp.int32), axis=1)
    slots = jnp.arange(CAP, dtype=jnp.int32)
    chosen = (holder[None, :] == lax.axis_index("dom")) & (order_rank[None, :] == slots[:, None])
    mine = jnp.dot(chosen.astype(F32), tile_vals, precision=EXACT)
    return (second, mine.reshape(CAP, 1, 2, TILE * TILE))


def solution(mesh):
    return jax.shard_map(
        local,
        mesh=mesh,
        in_specs=(
            P("dom", "band"),
            P("dom"),
            P(None, "dom"),
            P(),
            P(),
            P(None, "dom"),
            P("dom"),
            P(),
        ),
        out_specs=(P("dom", "band"), P("dom", "band", None, None)),
        check_vma=False,
    )
```

time: 2240 us -> 986 us (0.44)
  other arithmetic: 744 us -> 9.32 us
  local copies, waits for them, and re-layouts: 613 us -> 23.6 us
  Pallas kernels: 0 us -> 261 us
  matrix products: 172 us -> 9.77 us
  waiting for transfers between devices: 661 us -> 625 us
    scatter-add x15 -> x0, other arithmetic: 669 us -> none  [the longest x12 622 us: layer_work(): totals.at[cell_nodes].add(result.reshape(NPC, layer_cells, state_count))]
    unnamed x3 -> x2, waiting for transfers between devices: 656 us -> 0.03 us
    psum x0 -> x1, waiting for transfers between devices: none -> 613 us  [local(): pair = lax.psum(pair * inverse, 'dom')]
    gather x15 -> x0, local copies, waits for them, and re-layouts: 430 us -> none  [the longest x12 413 us: layer_work(): cell_vals = source[cell_nodes].reshape(NPC, layer_cells * state_count)]
    pallas_call x0 -> x4, Pallas kernels: none -> 261 us  [the longest x3 252 us: operate(): pl.pallas_call(functools.partial(apply_kernel, which, sizes), out_shape=o...]
    dot_general x27 -> x3, matrix products: 172 us -> 9.77 us  [the longest x2 8.61 us: project(): lax.dot_general(columns, mine, (((0,), (0,)), ((), ())), preferred_elemen...]
    reshape x25 -> x3, local copies, waits for them, and re-layouts: 99.1 us -> 1.15 us  [the longest x2 0.66 us: local(): pair.reshape(tile_rows, TILE, 2, tile_cols, TILE).transpose(0, 3, 2, 1, 4)]
    mul x12 -> x0, local copies, waits for them, and re-layouts: 40.2 us -> none  [layer_work(): quad_pot[:, :, None] * at_points]
  transfers between devices with their start and end apart: 8 -> 8, of which waited for: 4 -> 5; matrix products, arithmetic and copies ran while one was open for 22% -> 1% of each run, Pallas kernels for 0% -> 9%
where the time goes in v1:
time: 986 us; the launch traced here: 985 us
  waiting for transfers between devices  625 us (63%)
  Pallas kernels  261 us (26%)
  starting transfers between devices  28.2 us (3%)
  local copies, waits for them, and re-layouts  23.6 us (2%)
  between operations  14.9 us (2%)
  blocking collectives  13.4 us (1%)
    psum x1, waiting for transfers between devices, local(): pair = lax.psum(pair * inverse, 'dom')  613 us
    pallas_call x3, Pallas kernels, operate(): pl.pallas_call(functools.partial(apply_kernel, which, sizes), out_shape=o...  252 us
    ppermute x6, starting transfers between devices, from_behind(): lax.ppermute(value, axis, [(source, source + steps) for source in range(i...  28.2 us
  transfers between devices with their start and end apart: 8, of which 5 were waited for; matrix products, arithmetic and copies ran while one was open for 1% of the time, Pallas kernels for 9%

profile of v1, /device:TPU:0, one launch (start us, length us, event | category | flops | bytes accessed | tf_op | source)
XLA Modules:
  0.0 985.4 jit_solution(14819281801672695747)
XLA Ops:
  7.2 0.0 all-gather.2.cloned.1.call-start
  7.2 0.9 pad.20
  8.1 6.0 pad.22.states.refs_7_.refs_10_
  14.1 8.1 pad.21.mass.refs_6_
  22.2 8.6 edge_rows.1
  30.8 1.4 multiply_convert_fusion.3
  32.2 1.3 collective-permute-start
  33.6 0.7 copy.21
  34.3 1.1 and_reduce_fusion
  36.1 0.7 pad.19.refs_3_
  36.8 0.7 copy.16
  37.5 0.6 copy-done.7
  38.1 0.1 copy-done.8
  38.2 79.8 %apply_1.1 = (bf16[16512,128]{1,0:T(8,128)(2,1)}, f32[1376,128]{1,0:T(8,128)}, bf16[1376,128]{1,0:T(8,128)(2,1)}) custom-call(s32[65536]{0:T(1024)} %bitcast.29, s32[1369]{0:T(1024)} %refs_1_.5, s32[1]{0:T(128)} %bitcast.1.refs_2_, f32[64,640]{1,0:T(8,128)} %pad.19.refs_3_, bf16[128,64]{1,0:T(8,128)(2,1)} %copy-done.7, bf16[64,64]{1,0:T(8,128)(2,1)} %bitcast.34, ...), custom_call_target="tpu_custom_call" | custom-call | tf_op jit(solution)/shard_map/apply_1/pallas_call | solution.py:308
  118.0 5.6 collective-permute-start.1
  123.7 1.5 collective-permute-done.1
  125.1 0.7 copy-done.4
  125.9 2.1 fusion.21
  128.0 1.3 collective-permute-start.2
  129.3 4.9 collective-permute-done.2.refs_8_
  134.2 0.7 copy-done.10
  134.9 82.1 %apply_2.1 = (bf16[16512,128]{1,0:T(8,128)(2,1)}, f32[1376,128]{1,0:T(8,128)}, bf16[1376,128]{1,0:T(8,128)(2,1)}) custom-call(s32[65536]{0:T(1024)} %bitcast.30, s32[1369]{0:T(1024)} %refs_1_.5, s32[1]{0:T(128)} %bitcast.1.refs_2_, f32[64,640]{1,0:T(8,128)} %pad.19.refs_3_, bf16[128,64]{1,0:T(8,128)(2,1)} %copy-done.7, bf16[64,64]{1,0:T(8,128)(2,1)} %bitcast.35, ...), custom_call_target="tpu_custom_call" | custom-call | tf_op jit(solution)/shard_map/apply_2/pallas_call | solution.py:308
  217.1 0.0 all-reduce.6.cloned.1.call-start
  217.1 0.9 copy-done.14
  218.0 8.2 collective-permute-start.3
  226.2 1.3 collective-permute-done.3
  227.4 2.3 fusion.18
  229.7 0.9 fusion.20
  230.6 1.3 collective-permute-start.4
  231.9 4.8 collective-permute-done.4.refs_8_
  236.7 0.7 copy-done.9
  237.4 90.2 %apply_3.1 = (bf16[16512,256]{1,0:T(8,128)(2,1)}, f32[1376,128]{1,0:T(8,128)}, bf16[1376,128]{1,0:T(8,128)(2,1)}, bf16[16428,128]{1,0:T(8,128)(2,1)}) custom-call(s32[65536]{0:T(1024)} %bitcast.31, s32[1369]{0:T(1024)} %refs_1_.5, s32[1]{0:T(128)} %bitcast.1.refs_2_, f32[64,640]{1,0:T(8,128)} %pad.19.refs_3_, bf16[128,64]{1,0:T(8,128)(2,1)} %copy-done.7, ...), custom_call_target="tpu_custom_call" | custom-call | tf_op jit(solution)/shard_map/apply_3/pallas_call | solution.py:308
  327.6 10.5 %collective-permute-start.5 = (bf16[1376,128]{1,0:T(8,128)(2,1)}, bf16[1376,128]{1,0:T(8,128)(2,1)S(1)}, u32[]{:S(2)}, u32[]{:S(2)}) collective-permute-start(bf16[1376,128]{1,0:T(8,128)(2,1)} %get-tuple-element.25), channel_id=1, source_target_pairs={{0,2},{2,4},{4,6},{6,8},{8,10},{10,12},{12,14},{14,16},{16,18},{18... | collective-permute-start | bytes 1056776 | tf_op jit(solution)/shard_map/ppermute | solution.py:37
  338.2 0.1 constant_dynamic-slice_fusion
  338.2 0.1 broadcast_in_dim_reshape.2
  338.3 13.4 %all_gather.7 = bf16[1376,256]{1,0:T(8,128)(2,1)S(1)} all-gather(bf16[1376,128]{1,0:T(8,128)(2,1)S(1)} %get-tuple-element.33), channel_id=1, replica_groups=mesh['dom'=64,'band'=2] {'band'}, dimensions={1}, use_global_device_ids=true | all-gather | bytes 1056768 | tf_op jit(solution)/shard_map/all_gather | solution.py:345
  351.8 1.2 multiply_convert_fusion
  353.0 0.4 fusion.5
  353.4 0.0 all-gather.2.cloned.1.call-done
  353.4 8.2 fusion
  361.6 0.5 reshape.57
  362.1 0.2 copy.24
  362.3 0.5 reshape.58
  362.8 0.7 copy.25
  363.5 0.2 convert_reduce_fusion
  363.7 613.0 %all-reduce.6.cloned.1.call-done = f32[2,1024,32]{1,2,0:T(8,128)} async-done(((f32[2,1024,32]{1,2,0:T(8,128)}), f32[2,1024,32]{1,2,0:T(8,128)}) %all-reduce.6.cloned.1.call-update) | async-done | bytes 262160 | tf_op jit(solution)/shard_map/psum | solution.py:363
  976.8 1.2 convolution_bitcast_fusion
  977.9 0.6 copy.19
  (35 shorter events, 0.2 us)
Async XLA Ops:
  7.2 331.0 %copy-start = (s32[8,8]{1,0:T(8,128)S(1)}, s32[8,8]{1,0:T(8,128)}, u32[]{:S(2)}) copy-start(s32[8,8]{1,0:T(8,128)} %param.15) | copy-start | bytes 772
  7.2 346.2 %all-gather.2.cloned.1.call-start = ((), (), s32[]{:S(2)}) async-start(), calls=%async_computation | async-start | bytes 12681216 | tf_op jit(solution)/shard_map/all_gather | solution.py:337
  22.2 11.3 %copy-start.6 = (s32[64,576]{1,0:T(8,128)S(1)}, s32[64,576]{1,0:T(8,128)}, u32[]{:S(2)}) copy-start(s32[64,576]{1,0:T(8,128)} %param.13) | copy-start | bytes 442372
  22.2 13.9 %copy-start.11 = (f32[64,576]{1,0:T(8,128)S(1)}, f32[64,576]{1,0:T(8,128)}, u32[]{:S(2)}) copy-start(f32[64,576]{1,0:T(8,128)} %param.10) | copy-start | bytes 442372
  22.2 14.6 %copy-start.12 = (bf16[64,64]{1,0:T(8,128)(2,1)S(1)}, bf16[64,64]{1,0:T(8,128)(2,1)}, u32[]{:S(2)}) copy-start(bf16[64,64]{1,0:T(8,128)(2,1)} %param.12) | copy-start | bytes 24580
  22.2 15.3 %copy-start.13 = (bf16[64,64]{1,0:T(8,128)(2,1)S(1)}, bf16[64,64]{1,0:T(8,128)(2,1)}, u32[]{:S(2)}) copy-start(bf16[64,64]{1,0:T(8,128)(2,1)} %param.11) | copy-start | bytes 24580
  32.2 5.3 collective-permute-start
  37.5 0.6 copy-start.7
  37.5 0.7 copy-start.8
  38.2 87.6 %copy-start.1 = (f32[1376,128]{1,0:T(8,128)S(1)}, f32[1376,128]{1,0:T(8,128)}, u32[]{:S(2)}) copy-start(f32[1376,128]{1,0:T(8,128)} %get-tuple-element.14) | copy-start | bytes 2113540
  38.2 87.6 %copy-start.2 = (f32[1376,128]{1,0:T(8,128)S(1)}, f32[1376,128]{1,0:T(8,128)}, u32[]{:S(2)}) copy-start(f32[1376,128]{1,0:T(8,128)} %get-tuple-element.15) | copy-start | bytes 2113540
  118.0 7.1 collective-permute-start.1
  125.1 0.7 copy-start.4
  128.0 6.2 collective-permute-start.2
  134.2 0.7 copy-start.10
  217.0 1.0 copy-start.14
  217.0 10.4 %copy-start.3 = (f32[1376,128]{1,0:T(8,128)S(1)}, f32[1376,128]{1,0:T(8,128)}, u32[]{:S(2)}) copy-start(f32[1376,128]{1,0:T(8,128)} %get-tuple-element.17) | copy-start | bytes 2113540
  217.0 10.4 %copy-start.5 = (bf16[1376,128]{1,0:T(8,128)(2,1)S(1)}, bf16[1376,128]{1,0:T(8,128)(2,1)}, u32[]{:S(2)}) copy-start(bf16[1376,128]{1,0:T(8,128)(2,1)} %copy-done.4) | copy-start | bytes 1056772
  217.1 759.7 %all-reduce.6.cloned.1.call-start = ((), (), s32[]{:S(2)}) async-start(), calls=%async_computation.1 | async-start | bytes 524288 | tf_op jit(solution)/shard_map/psum | solution.py:363
  218.0 9.4 collective-permute-start.3
  230.6 6.1 collective-permute-start.4
  236.7 0.7 copy-start.9
  327.6 24.1 %collective-permute-start.5 = (bf16[1376,128]{1,0:T(8,128)(2,1)}, bf16[1376,128]{1,0:T(8,128)(2,1)S(1)}, u32[]{:S(2)}, u32[]{:S(2)}) collective-permute-start(bf16[1376,128]{1,0:T(8,128)(2,1)} %get-tuple-element.25), channel_id=1, source_target_pairs={{0,2},{2,4},{4,6},{6,8},{8,10},{10,12},{12,14},{14,16},{16,18},{18... | collective-permute-start | bytes 1056776 | tf_op jit(solution)/shard_map/ppermute | solution.py:37
Sparse Core Ops, SparseCore 0:
  217.2 129.5 all-gather.1
  363.6 613.0 all-reduce.5

commit v2 on v1

v2 whole, which is shorter than its diff:
```python
import functools

import jax
import jax.numpy as jnp
from jax import lax
from jax.experimental import pallas as pl
from jax.experimental.pallas import tpu as pltpu
from jax.sharding import PartitionSpec as P

NPC = 64
QP = 64
TILE = 32
CAP = 4
CENTER = 1.0
INV_HALF = 0.25
EXACT = lax.Precision.HIGHEST
DIMS = (2, 4, 4, 2)

LANES = 128
ROWS = 128
GROUP = 4
TURN = 2 * GROUP
BATCH = 8
SCOPED = 30
STRIDE = 1024
F32 = jnp.float32
BF16 = jnp.bfloat16
VMEM = pl.BlockSpec(memory_space=pltpu.VMEM)
SMEM = pl.BlockSpec(memory_space=pltpu.SMEM)
ANY = pl.BlockSpec(memory_space=pl.ANY)


def round_up(count, unit):
    return -(-count // unit) * unit


def from_behind(value, axis, steps):
    count = lax.axis_size(axis)
    initial, last = (max(0, -steps), min(count, count - steps))
    return lax.ppermute(value, axis, [(source, source + steps) for source in range(initial, last)])


def params(mebibytes):
    return pltpu.CompilerParams(vmem_limit_bytes=mebibytes << 20)


def cost(us):
    return pl.CostEstimate(flops=us * 10**9, bytes_accessed=us * 10**6, transcendentals=0)


def by_rows(count, work):
    def step(i, _):
        work(pl.ds(pl.multiple_of(i * ROWS, ROWS), ROWS))
        return 0

    lax.fori_loop(0, count // ROWS, step, 0)


def by_entries(count, work):
    unroll = max(u for u in range(1, 65) if count % u == 0)

    def step(i, _):
        for j in range(unroll):
            work(i * unroll + j)
        return 0

    lax.fori_loop(0, count // unroll, step, 0)


def gather(src, lists, cells, out):
    for k, cell in enumerate(cells):
        for j in range(NPC):
            out[k * NPC + j : k * NPC + j + 1, :] = src[pl.ds(lists[j][cell], 1), :]


def multiply(vals, pot, base, stacked, basis_t, out):
    chunk = pl.multiple_of((base // LANES) * LANES, LANES)
    shift = lax.rem(LANES - lax.rem(base, LANES), LANES)
    columns = pltpu.roll(pot[:, pl.ds(chunk, LANES)], shift, 1)
    for p in range(0, GROUP, 2):
        pair = jnp.concatenate(
            [vals[k * NPC : (k + 1) * NPC, :] for k in (p, p + 1)], axis=1
        ).astype(BF16)
        both = jnp.dot(stacked, pair, preferred_element_type=F32)
        weight = jnp.concatenate(
            [jnp.broadcast_to(columns[:, k : k + 1], (QP, LANES)) for k in (p, p + 1)], axis=1
        )
        weighted = (weight * both[:QP]).astype(BF16)
        result = jnp.dot(basis_t, weighted, preferred_element_type=F32) + both[QP:]
        for k in (p, p + 1):
            out[k * NPC : (k + 1) * NPC, :] = result[:, (k - p) * LANES : (k - p + 1) * LANES]


def scatter(res, lists, cells, sums, batch):
    for p in range(0, GROUP, 2):
        for start in range(0, NPC, batch):
            moved = []
            for k in (p, p + 1):
                for j in range(start, start + batch):
                    row = pl.ds(lists[j][cells[k]], 1)
                    total = sums[k - p][row, :] + res[k * NPC + j : k * NPC + j + 1, :]
                    moved.append((k - p, row, total))
            for which, row, total in moved:
                sums[which][row, :] = total


def cells_of(group):
    return [group * GROUP + k for k in range(GROUP)]


def sweep(begin, end, repeated, src, lists, pot, stacked_ref, basis_t_ref, sums, vals, ress):
    def mult(slot, group, stacked, basis_t):
        multiply(vals[slot], pot, group * GROUP, stacked, basis_t, ress[slot])

    def two(i, _):
        stacked, basis_t = stacked_ref[...], basis_t_ref[...]
        first = 2 * i
        gather(src, lists, cells_of(first + 1), vals[1])
        mult(0, first, stacked, basis_t)
        scatter(ress[1], lists, cells_of(jnp.maximum(first - 1, 2 * begin)), sums, BATCH)
        gather(src, lists, cells_of(jnp.minimum(first + 2, 2 * end - 1)), vals[0])
        mult(1, first + 1, stacked, basis_t)
        scatter(ress[0], lists, cells_of(first), sums, BATCH)
        return 0

    @pl.when((end > begin) & (repeated == 0))
    def _():
        ress[1][...] = jnp.zeros_like(ress[1])
        gather(src, lists, cells_of(2 * begin), vals[0])
        lax.fori_loop(begin, end, two, 0)
        scatter(ress[1], lists, cells_of(2 * end - 1), sums, BATCH)

    @pl.when((end > begin) & (repeated != 0))
    def _():
        def one(i, _):
            gather(src, lists, cells_of(i), vals[0])
            mult(0, i, stacked_ref[...], basis_t_ref[...])
            scatter(ress[0], lists, cells_of(i), sums, 1)
            return 0

        lax.fori_loop(2 * begin, 2 * end, one, 0)


def start_kernel(
    edge_count, edge, states, mass_rows, mass, kept, src, sum_a, sum_b, states_edge, mass_edge, sent
):
    nodes = states.shape[0]
    padded = kept.shape[0]
    whole = nodes // ROWS * ROWS

    def widen(rows):
        sum_a[rows, :] = states[rows, :].astype(F32)

    by_rows(whole, widen)
    if whole < padded:
        sum_a[whole:padded, :] = jnp.zeros((padded - whole, LANES), F32)
        sum_a[whole:nodes, :] = states[whole:nodes, :].astype(F32)

    def scale(i, _):
        rows = pl.ds(pl.multiple_of(i * ROWS, ROWS), ROWS)
        column = jnp.broadcast_to(mass_rows[pl.ds(i, 1), :], (ROWS, LANES)).T
        value = sum_a[rows, :]
        mass[rows, :] = column
        kept[rows, :] = value.astype(BF16)
        src[rows, :] = (column * value).astype(BF16).astype(F32)
        return 0

    lax.fori_loop(0, padded // ROWS, scale, 0)
    tail = states_edge.shape[0] - 8
    states_edge[tail:, :] = jnp.zeros((8, LANES), F32)
    mass_edge[tail:, :] = jnp.zeros((8, LANES), F32)

    def take(i):
        row = pl.ds(edge[i], 1)
        states_edge[pl.ds(i, 1), :] = sum_a[row, :]
        mass_edge[pl.ds(i, 1), :] = mass[row, :]

    by_entries(edge_count, take)
    sent[...] = (mass_edge[...] * states_edge[...]).astype(BF16)
    src[padded:, :] = jnp.zeros((src.shape[0] - padded, LANES), F32)

    def clear(rows):
        sum_a[rows, :] = jnp.zeros((ROWS, LANES), F32)
        sum_b[rows, :] = jnp.zeros((ROWS, LANES), F32)

    by_rows(sum_a.shape[0], clear)


def cells_kernel(part, which, edge_count, padded, *refs):
    refs = list(refs)
    conn, counts, pot, stacked, basis_t, src, sum_a, sum_b = refs[:8]
    refs = refs[8:]
    if part == 0 and which > 1:
        edge, scaled_edge = refs[:2]
        refs = refs[2:]
    if part == 1:
        ghost = refs.pop(0)
    sources = []
    if part == 2:
        edge = refs.pop(0)
        if which == 3:
            second_edge = refs.pop(0)
        loads = 3 if which == 2 else 2
        sources, refs = refs[:loads], refs[loads:]
    refs = refs[3:]
    if part == 1:
        outgoing = refs.pop(0)
    if part == 2:
        edge_sums, result = refs[:2]
        refs = refs[2:]
        if which == 3:
            second = refs.pop(0)
    val_a, val_b, res_a, res_b, arrived = refs[:5]
    lists, refs = refs[5 : 5 + NPC], refs[5 + NPC :]
    if part == 2:
        loaded, refs = refs[0], refs[1:]
        fetches = [
            pltpu.make_async_copy(source, ref, loaded.at[n])
            for n, (source, ref) in enumerate(zip(sources, refs))
        ]
    copies = [
        pltpu.make_async_copy(conn.at[pl.ds(j * STRIDE, STRIDE)], lists[j], arrived.at[j])
        for j in range(NPC)
    ]
    for copy in copies:
        copy.start()
    if part == 2:
        for fetch in fetches:
            fetch.start()
    if part == 0 and which > 1:

        def patch(i):
            src[pl.ds(edge[i], 1), :] = scaled_edge[pl.ds(i, 1), :]

        by_entries(edge_count, patch)
    if part == 1:
        src[padded : padded + ghost.shape[0], :] = ghost[...].astype(F32)
    for copy in copies:
        copy.wait()

    begin, end = ((0, counts[0]), (counts[1], counts[2]), (counts[0], counts[1]))[part]
    sums = (sum_a, sum_b)
    sweep(
        begin,
        end,
        counts[3],
        src,
        lists,
        pot,
        stacked,
        basis_t,
        sums,
        (val_a, val_b),
        (res_a, res_b),
    )
    if part == 1:
        ghost_rows = slice(padded, padded + ghost.shape[0])
        outgoing[...] = (sum_a[ghost_rows, :] + sum_b[ghost_rows, :]).astype(BF16)
        blank = jnp.zeros(ghost.shape, F32)
        sum_a[ghost_rows, :] = blank
        sum_b[ghost_rows, :] = blank
    if part < 2:
        return

    for fetch in fetches:
        fetch.wait()
    mass, values = refs[:2]
    tail = edge_sums.shape[0] - 8
    edge_sums[tail:, :] = jnp.zeros((8, LANES), F32)

    def take(i):
        row = pl.ds(edge[i], 1)
        edge_sums[pl.ds(i, 1), :] = sum_a[row, :] + sum_b[row, :]
        if which == 3:
            sum_a[row, :] = jnp.zeros((1, LANES), F32)
            sum_b[row, :] = jnp.zeros((1, LANES), F32)

    by_entries(edge_count, take)

    def finish(rows):
        scale = mass[rows, :]
        image = scale * (sum_a[rows, :] + sum_b[rows, :])
        value = values[rows, :].astype(F32)
        if which == 3:
            result[rows, :LANES] = image.astype(BF16)
            src[rows, :] = value
            return
        if which == 1:
            after = ((image - CENTER * value) * INV_HALF).astype(BF16)
        else:
            start = refs[2][rows, :].astype(F32)
            after = (2.0 * INV_HALF * (image - CENTER * value) - start).astype(BF16)
        result[rows, :] = after
        src[rows, :] = (scale * after.astype(F32)).astype(BF16).astype(F32)
        sum_a[rows, :] = jnp.zeros((ROWS, LANES), F32)
        sum_b[rows, :] = jnp.zeros((ROWS, LANES), F32)

    by_rows(padded, finish)
    if which == 3:

        def blank(i):
            src[pl.ds(edge[i], 1), :] = jnp.zeros((1, LANES), F32)

        def fill(i):
            src[pl.ds(edge[i], 1), :] = second_edge[pl.ds(i, 1), :]

        def blanked(rows):
            result[rows, LANES:] = src[rows, :].astype(BF16)

        def filled(rows):
            second[rows, :] = src[rows, :].astype(BF16)

        nodes = second.shape[0]
        by_entries(edge_count, blank)
        by_rows(padded, blanked)
        by_entries(edge_count, fill)
        whole = nodes // ROWS * ROWS
        by_rows(whole, filled)
        if whole < nodes:
            second[whole:nodes, :] = src[whole:nodes, :].astype(BF16)


def arrange(connectivity, potential, node_count, padded):
    cell_count = connectivity.shape[1]
    is_ghost = connectivity >= node_count
    late = jnp.any(is_ghost, axis=0).astype(F32)[None]
    before = jnp.triu(jnp.ones((cell_count, cell_count), F32), 1)
    ranks = jnp.dot(jnp.concatenate([late, 1.0 - late], 0), before, precision=EXACT)
    late_count = jnp.sum(late).astype(jnp.int32)
    turns = (cell_count - late_count + TURN - 1) // TURN
    late_turns = (late_count + TURN - 1) // TURN
    place = jnp.where(late[0] > 0, (turns * TURN).astype(F32) + ranks[0], ranks[1])
    slots = round_up(round_up(cell_count, TURN) + TURN, LANES)
    hot = (place[:, None] == jnp.arange(slots, dtype=F32)[None, :]).astype(F32)
    moved = jnp.dot(
        jnp.concatenate([connectivity.astype(F32), potential], 0), hot, precision=EXACT
    )
    index = jnp.round(moved[:NPC]).astype(jnp.int32)
    index = jnp.where(index >= node_count, index + (padded - node_count), index)
    used = jnp.sum(hot, axis=0) > 0
    spare = node_count + jnp.arange(NPC, dtype=jnp.int32)
    index = jnp.where(used[None, :], index, spare[:, None])
    lists = jnp.pad(index, ((0, 0), (0, STRIDE - slots))).reshape(-1)

    batched = jnp.where(is_ghost, connectivity, -1).reshape(NPC // BATCH, BATCH, cell_count)
    same = (batched[:, :, None] == batched[:, None, :]) & (batched[:, :, None] >= 0)
    apart = ~jnp.eye(BATCH, dtype=bool)[None, :, :, None]
    repeated = jnp.any(same & apart).astype(jnp.int32)
    counts = jnp.stack([turns // 2, turns, turns + late_turns, repeated])
    return lists, moved[NPC:], counts


def swap(value, dim, offset):
    step = 1
    for size in DIMS[dim + 1 :]:
        step *= size
    count, total = DIMS[dim], lax.axis_size("dom")
    pairs = []
    for source in range(total):
        digit = source // step % count
        pairs.append((source, source + ((digit + offset) % count - digit) * step))
    return lax.ppermute(value, "dom", pairs)


def to_owners(tiles, holder):
    here = lax.axis_index("dom")

    def digits(index):
        found = []
        for size in reversed(DIMS):
            found.append(index % size)
            index = index // size
        return found[::-1]

    mine, owner = digits(here), digits(holder)
    count = holder.shape[0]
    before = jnp.arange(count)[:, None] < jnp.arange(count)[None, :]

    def chosen(member, slots):
        rank = jnp.sum((member[:, None] & before).astype(jnp.int32), axis=0)
        return (member[None, :] & (rank[None, :] == jnp.arange(slots)[:, None])).astype(F32)

    column = (owner[0] == mine[0]) & (owner[3] == mine[3])
    plane_slots = min(count, DIMS[1] * CAP)
    for_plane = [
        chosen(column & (owner[2] == (mine[2] + k) % DIMS[2]), plane_slots)
        for k in range(DIMS[2])
    ]
    for_row = [
        chosen(column & (owner[2] == mine[2]) & (owner[1] == (mine[1] + k) % DIMS[1]), CAP)
        for k in range(DIMS[1])
    ]
    by_row = jnp.einsum("kst,ut->ksu", jnp.stack(for_row), for_plane[0], precision=EXACT)
    tiles = tiles + swap(tiles, 3, 1)
    tiles = tiles + swap(tiles, 0, 1)
    parts = jnp.dot(jnp.concatenate(for_plane, 0), tiles, precision=EXACT)
    parts = parts.reshape(DIMS[2], plane_slots, tiles.shape[1])
    total = parts[0]
    for arrived in [swap(parts[k], 2, k) for k in range(1, DIMS[2])]:
        total = total + arrived
    parts = jnp.dot(by_row.reshape(DIMS[1] * CAP, plane_slots), total, precision=EXACT)
    parts = parts.reshape(DIMS[1], CAP, tiles.shape[1])
    total = parts[0]
    for arrived in [swap(parts[k], 1, k) for k in range(1, DIMS[1])]:
        total = total + arrived
    return total


def local(states, mass_scale, potential, kinetic, basis_fn, connectivity, boundary, owners):
    node_count, state_count = states.shape
    edge_count = boundary.shape[0]
    padded = round_up(node_count + NPC, ROWS)
    edge_rows = round_up(edge_count + 7, 16)
    total_rows = round_up(padded + edge_rows, ROWS)

    wide = pltpu.VMEM((total_rows, LANES), F32)
    edge_shape = jax.ShapeDtypeStruct((edge_rows, LANES), F32)
    edge_half = jax.ShapeDtypeStruct((edge_rows, LANES), BF16)
    padded_half = jax.ShapeDtypeStruct((padded, LANES), BF16)
    both_half = jax.ShapeDtypeStruct((padded, 2 * LANES), BF16)
    whole_half = jax.ShapeDtypeStruct((node_count, LANES), BF16)

    mass_rows = jnp.pad(mass_scale, (0, padded - node_count)).reshape(padded // ROWS, ROWS)
    mass, kept, src, sum_a, sum_b, states_edge, mass_edge, sent = pl.pallas_call(
        functools.partial(start_kernel, edge_count),
        out_shape=(jax.ShapeDtypeStruct((padded, LANES), F32), padded_half, wide, wide, wide)
        + (edge_shape, edge_shape, edge_half),
        in_specs=[SMEM, VMEM, VMEM],
        out_specs=(VMEM,) * 8,
        compiler_params=params(SCOPED),
        cost_estimate=cost(10),
        name="start",
    )(boundary, states, mass_rows)
    ghost = from_behind(sent, "dom", -1)
    lists, pot, counts = arrange(connectivity, potential, node_count, padded)
    stacked = jnp.concatenate([basis_fn, kinetic], 0)
    basis_t = basis_fn.T
    block = pltpu.VMEM((GROUP * NPC, LANES), F32)

    def cells(part, which, held, specs, extra, outs, scratch=()):
        return pl.pallas_call(
            functools.partial(cells_kernel, part, which, edge_count, padded),
            out_shape=(wide, wide, wide) + outs,
            in_specs=[ANY, SMEM] + [VMEM] * 6 + specs,
            out_specs=(VMEM,) * (3 + len(outs)),
            input_output_aliases={5: 0, 6: 1, 7: 2},
            scratch_shapes=[block, block, block, block]
            + [pltpu.SemaphoreType.DMA((NPC,))]
            + [pltpu.SMEM((STRIDE,), jnp.int32)] * NPC
            + list(scratch),
            compiler_params=params(SCOPED),
            cost_estimate=cost(20),
            name=f"cells_{which}_{part}",
        )(lists, counts, pot, stacked, basis_t, *held, *extra)

    def joined(edge_sums, outgoing):
        incoming = from_behind(outgoing, "dom", 1)
        return mass_edge * (edge_sums + incoming.astype(F32))

    def scaled(edge):
        return (mass_edge * edge).astype(BF16)

    loaded = pltpu.SemaphoreType.DMA((3,))
    mass_room = pltpu.VMEM((padded, LANES), F32)
    half_room = pltpu.VMEM((padded, LANES), BF16)
    held = cells(0, 1, (src, sum_a, sum_b), [], (), ())
    *held, outgoing = cells(1, 1, held, [VMEM], (ghost,), (edge_half,))
    *held, sums, one = cells(
        2,
        1,
        held,
        [SMEM, ANY, ANY],
        (boundary, mass, kept),
        (edge_shape, padded_half),
        (loaded, mass_room, half_room),
    )
    one_edge = ((joined(sums, outgoing) - CENTER * states_edge) * INV_HALF).astype(BF16).astype(F32)

    sent = scaled(one_edge)
    ghost = from_behind(sent, "dom", -1)
    held = cells(0, 2, held, [SMEM, VMEM], (boundary, sent.astype(F32)), ())
    *held, outgoing = cells(1, 2, held, [VMEM], (ghost,), (edge_half,))
    *held, sums, two = cells(
        2,
        2,
        held,
        [SMEM, ANY, ANY, ANY],
        (boundary, mass, one, kept),
        (edge_shape, padded_half),
        (loaded, mass_room, half_room, half_room),
    )
    turned = [(0, 1), (1, 0)]
    other = lax.ppermute(two, "band", turned)
    two_half = (
        2.0 * INV_HALF * (joined(sums, outgoing) - CENTER * one_edge) - states_edge
    ).astype(BF16)
    two_edge = two_half.astype(F32)
    other_edge = lax.ppermute(two_half, "band", turned)

    sent = scaled(two_edge)
    ghost = from_behind(sent, "dom", -1)
    held = cells(0, 3, held, [SMEM, VMEM], (boundary, sent.astype(F32)), ())
    *held, outgoing = cells(1, 3, held, [VMEM], (ghost,), (edge_half,))
    *held, sums, own, second = cells(
        2,
        3,
        held,
        [SMEM, VMEM, ANY, ANY],
        (boundary, two_edge, mass, two),
        (edge_shape, both_half, whole_half),
        (loaded, mass_room, half_room),
    )
    image_edge = joined(sums, outgoing).astype(BF16)
    own_edge = jnp.concatenate([image_edge, two_half], 1)

    def project(columns, mine):
        return lax.dot_general(
            columns, mine, (((0,), (0,)), ((), ())), preferred_element_type=F32
        )

    inverse = 1.0 / (node_count * lax.axis_size("dom"))
    near = (project(two, own) + project(two_half, own_edge)) * inverse
    far = (project(other, own) + project(other_edge, own_edge)) * inverse
    lower = lax.axis_index("band") == 0
    pair = jnp.concatenate([jnp.where(lower, near, far), jnp.where(lower, far, near)], 0)

    tile_rows = pair.shape[0] // TILE
    tile_cols = state_count // TILE
    tile_count = tile_rows * tile_cols
    tile_vals = (
        pair.reshape(tile_rows, TILE, 2, tile_cols, TILE)
        .transpose(0, 3, 2, 1, 4)
        .reshape(tile_count, 2 * TILE * TILE)
    )
    holder = lax.dynamic_slice_in_dim(
        owners, lax.axis_index("band") * tile_cols, tile_cols, 1
    ).reshape(tile_count)
    mine = to_owners(tile_vals, holder)
    return (second, mine.reshape(CAP, 1, 2, TILE * TILE))


def solution(mesh):
    return jax.shard_map(
        local,
        mesh=mesh,
        in_specs=(
            P("dom", "band"),
            P("dom"),
            P(None, "dom"),
            P(),
            P(),
            P(None, "dom"),
            P("dom"),
            P(),
        ),
        out_specs=(P("dom", "band"), P("dom", "band", None, None)),
        check_vma=False,
    )
```

time: 986 us -> 511 us (0.52)
  waiting for transfers between devices: 625 us -> 19.3 us
  starting transfers between devices: 28.2 us -> 101 us
  Pallas kernels: 261 us -> 310 us
  local copies, waits for them, and re-layouts: 23.6 us -> 52.5 us
  blocking collectives: 13.4 us -> 0 us
  between operations: 14.9 us -> 2.77 us
    psum x1 -> x0, waiting for transfers between devices: 613 us -> none  [local(): pair = lax.psum(pair * inverse, 'dom')]
    ppermute x0 -> x10, starting transfers between devices: none -> 86.7 us  [the longest x8 84.6 us: swap(): return lax.ppermute(value, 'dom', pairs)]
    pallas_call x4 -> x10, Pallas kernels: 261 us -> 310 us  [the longest x9 285 us: cells(): pl.pallas_call(functools.partial(cells_kernel, part, which, edge_count, p...]
    unnamed x35 -> x88, local copies, waits for them, and re-layouts: 5.97 us -> 48.3 us
    ppermute x0 -> x10, waiting for transfers between devices: none -> 19.3 us  [the longest x8 19.3 us: swap(): return lax.ppermute(value, 'dom', pairs)]
    pad x4 -> x0, local copies, waits for them, and re-layouts: 15.6 us -> none  [the longest x2 8.99 us: local(): jnp.pad(jnp.broadcast_to(mass_scale[:, None], (node_count, LANES)), ((0,...]
    ppermute x6, starting transfers between devices: 28.2 us -> 14.6 us  [from_behind(): lax.ppermute(value, axis, [(source, source + steps) for source in range(i...]
    all_gather x1 -> x0, blocking collectives: 13.4 us -> none  [local(): edge_cols = lax.all_gather(two_half, 'band', axis=1, tiled=True)]
  transfers between devices with their start and end apart: 8 -> 16, of which waited for: 5 -> 7; matrix products, arithmetic and copies ran while one was open for 1% -> 3% of each run, Pallas kernels for 9% -> 47%
where the time goes in v2:
time: 511 us; the launch traced here: 510 us
  Pallas kernels  310 us (61%)
  starting transfers between devices  101 us (20%)
  local copies, waits for them, and re-layouts  52.5 us (10%)
  waiting for transfers between devices  19.3 us (4%)
  other arithmetic  14.4 us (3%)
  matrix products  9.56 us (2%)
    pallas_call x9, Pallas kernels, cells(): pl.pallas_call(functools.partial(cells_kernel, part, which, edge_count, p...  285 us
    ppermute x8, starting transfers between devices, swap(): return lax.ppermute(value, 'dom', pairs)  84.6 us
    unnamed x88, local copies, waits for them, and re-layouts  48.3 us
    pallas_call x1, Pallas kernels, local(): pl.pallas_call(functools.partial(start_kernel, edge_count), out_shape=(ja...  24.8 us
    ppermute x8, waiting for transfers between devices, swap(): return lax.ppermute(value, 'dom', pairs)  19.3 us
    ppermute x6, starting transfers between devices, from_behind(): lax.ppermute(value, axis, [(source, source + steps) for source in range(i...  14.6 us
  transfers between devices with their start and end apart: 16, of which 7 were waited for; matrix products, arithmetic and copies ran while one was open for 3% of the time, Pallas kernels for 47%

profile of v2, /device:TPU:0, one launch (start us, length us, event | category | flops | bytes accessed | tf_op | source)
XLA Modules:
  0.0 509.9 jit_solution(5358935394043195290)
XLA Ops:
  0.6 1.5 pad_bitcast_fusion.1.mass_rows
  2.2 24.8 %start.1 = (f32[16512,128]{1,0:T(8,128)}, bf16[16512,128]{1,0:T(8,128)(2,1)}, f32[17920,128]{1,0:T(8,128)S(1)}, f32[17920,128]{1,0:T(8,128)S(1)}, f32[17920,128]...) custom-call(s32[1369]{0:T(1024)} %refs_8_.9, bf16[16428,128]{1,0:T(8,128)(2,1)} %states.1, ...), custom_call_target="tpu_custom_call" | custom-call | flops 10000000000 | bytes 10000000 | tf_op jit(solution)/shard_map/start/pallas_call | solution.py:424
  27.0 3.6 copy-done.2
  30.5 3.6 copy-done.6
  34.1 3.6 copy-done.10
  37.7 1.3 collective-permute-start
  44.4 1.1 and_reduce_fusion
  50.0 3.6 copy-done.3
  53.6 3.6 copy-done.7
  57.2 3.7 copy-done.11
  60.8 30.0 %cells_1_0.1 = (f32[17920,128]{1,0:T(8,128)S(1)}, f32[17920,128]{1,0:T(8,128)S(1)}, f32[17920,128]{1,0:T(8,128)S(1)}) custom-call(s32[65536]{0:T(1024)} %bitcast.36, s32[4]{0:T(128)} %pad_add_fusion.refs_1_, f32[64,640]{1,0:T(8,128)} %slice.59.refs_2_, bf16[128,64]{1,0:T(8,128)(2,1)} %copy-done.22, ...), custom_call_target="tpu_custom_call", output_to_operand_aliasing={{0}: (5, {}), {1}: (6, {}), {2}: (7, {})} | custom-call | flops 20000000000 | bytes 20000000 | tf_op jit(solution)/shard_map/cells_1_0/pallas_call | solution.py:441
  90.9 3.6 copy-done.4
  94.4 3.6 copy-done.8
  98.0 3.6 copy-done.12
  104.3 3.6 copy-done.5
  107.9 3.6 copy-done.9
  111.5 3.7 copy-done.13
  115.2 23.4 %cells_1_1.1 = (f32[17920,128]{1,0:T(8,128)S(1)}, f32[17920,128]{1,0:T(8,128)S(1)}, f32[17920,128]{1,0:T(8,128)S(1)}, bf16[1376,128]{1,0:T(8,128)(2,1)}) custom-call(s32[65536]{0:T(1024)} %bitcast.37, s32[4]{0:T(128)} %pad_add_fusion.refs_1_, f32[64,640]{1,0:T(8,128)} %slice.59.refs_2_, ...), custom_call_target="tpu_custom_call", output_to_operand_aliasing={{0}: (5, {}), {1}: (6, {}), {2}: (7, {})} | custom-call | flops 20000000000 | bytes 20000000 | tf_op jit(solution)/shard_map/cells_1_1/pallas_call | solution.py:441
  138.5 3.0 collective-permute-start.1
  141.6 37.7 %cells_1_2.1 = (f32[17920,128]{1,0:T(8,128)S(1)}, f32[17920,128]{1,0:T(8,128)S(1)}, f32[17920,128]{1,0:T(8,128)S(1)}, f32[1376,128]{1,0:T(8,128)}, bf16[16512,128]{1,0:T(8,128)(2,1)}) custom-call(s32[65536]{0:T(1024)} %bitcast.38, s32[4]{0:T(128)} %pad_add_fusion.refs_1_, ...), custom_call_target="tpu_custom_call", output_to_operand_aliasing={{0}: (5, {}), {1}: (6, {}), {2}: (7, {})} | custom-call | flops 20000000000 | bytes 20000000 | tf_op jit(solution)/shard_map/cells_1_2/pallas_call | solution.py:441
  179.3 2.1 fusion.78
  181.4 1.3 collective-permute-start.2
  182.7 30.5 %cells_2_0.1 = (f32[17920,128]{1,0:T(8,128)S(1)}, f32[17920,128]{1,0:T(8,128)S(1)}, f32[17920,128]{1,0:T(8,128)S(1)}) custom-call(s32[65536]{0:T(1024)} %bitcast.39, s32[4]{0:T(128)} %pad_add_fusion.refs_1_, f32[64,640]{1,0:T(8,128)} %slice.59.refs_2_, bf16[128,64]{1,0:T(8,128)(2,1)} %copy-done.22, ...), custom_call_target="tpu_custom_call", output_to_operand_aliasing={{0}: (5, {}), {1}: (6, {}), {2}: (7, {})} | custom-call | flops 20000000000 | bytes 20000000 | tf_op jit(solution)/shard_map/cells_2_0/pallas_call | solution.py:441
  214.0 23.4 %cells_2_1.1 = (f32[17920,128]{1,0:T(8,128)S(1)}, f32[17920,128]{1,0:T(8,128)S(1)}, f32[17920,128]{1,0:T(8,128)S(1)}, bf16[1376,128]{1,0:T(8,128)(2,1)}) custom-call(s32[65536]{0:T(1024)} %bitcast.40, s32[4]{0:T(128)} %pad_add_fusion.refs_1_, f32[64,640]{1,0:T(8,128)} %slice.59.refs_2_, ...), custom_call_target="tpu_custom_call", output_to_operand_aliasing={{0}: (5, {}), {1}: (6, {}), {2}: (7, {})} | custom-call | flops 20000000000 | bytes 20000000 | tf_op jit(solution)/shard_map/cells_2_1/pallas_call | solution.py:441
  237.3 4.1 collective-permute-start.3
  241.5 38.3 %cells_2_2.1 = (f32[17920,128]{1,0:T(8,128)S(1)}, f32[17920,128]{1,0:T(8,128)S(1)}, f32[17920,128]{1,0:T(8,128)S(1)}, f32[1376,128]{1,0:T(8,128)}, bf16[16512,128]{1,0:T(8,128)(2,1)}) custom-call(s32[65536]{0:T(1024)} %bitcast.41, s32[4]{0:T(128)} %pad_add_fusion.refs_1_, ...), custom_call_target="tpu_custom_call", output_to_operand_aliasing={{0}: (5, {}), {1}: (6, {}), {2}: (7, {})} | custom-call | flops 20000000000 | bytes 20000000 | tf_op jit(solution)/shard_map/cells_2_2/pallas_call | solution.py:441
  279.7 1.6 collective-permute-start.6
  281.3 2.2 fusion.75
  283.6 0.9 fusion.77
  285.0 1.3 collective-permute-start.4
  286.3 30.3 %cells_3_0.1 = (f32[17920,128]{1,0:T(8,128)S(1)}, f32[17920,128]{1,0:T(8,128)S(1)}, f32[17920,128]{1,0:T(8,128)S(1)}) custom-call(s32[65536]{0:T(1024)} %bitcast.42, s32[4]{0:T(128)} %pad_add_fusion.refs_1_, f32[64,640]{1,0:T(8,128)} %slice.59.refs_2_, bf16[128,64]{1,0:T(8,128)(2,1)} %copy-done.22, ...), custom_call_target="tpu_custom_call", output_to_operand_aliasing={{0}: (5, {}), {1}: (6, {}), {2}: (7, {})} | custom-call | flops 20000000000 | bytes 20000000 | tf_op jit(solution)/shard_map/cells_3_0/pallas_call | solution.py:441
  317.4 23.4 %cells_3_1.1 = (f32[17920,128]{1,0:T(8,128)S(1)}, f32[17920,128]{1,0:T(8,128)S(1)}, f32[17920,128]{1,0:T(8,128)S(1)}, bf16[1376,128]{1,0:T(8,128)(2,1)}) custom-call(s32[65536]{0:T(1024)} %bitcast.43, s32[4]{0:T(128)} %pad_add_fusion.refs_1_, f32[64,640]{1,0:T(8,128)} %slice.59.refs_2_, ...), custom_call_target="tpu_custom_call", output_to_operand_aliasing={{0}: (5, {}), {1}: (6, {}), {2}: (7, {})} | custom-call | flops 20000000000 | bytes 20000000 | tf_op jit(solution)/shard_map/cells_3_1/pallas_call | solution.py:441
  340.8 3.7 collective-permute-start.5
  344.4 48.4 %cells_3_2.1 = (f32[17920,128]{1,0:T(8,128)S(1)}, f32[17920,128]{1,0:T(8,128)S(1)}, f32[17920,128]{1,0:T(8,128)S(1)}, f32[1376,128]{1,0:T(8,128)}, bf16[16512,25...) custom-call(s32[65536]{0:T(1024)} %bitcast.44, ...), custom_call_target="tpu_custom_call", output_to_operand_aliasing={{0}: (5, {}), {1}: (6, {}), {2}: (7, {})} | custom-call | flops 20000000000 | bytes 20000000 | tf_op jit(solution)/shard_map/cells_3_2/pallas_call | solution.py:441
  392.9 1.2 multiply_convert_fusion
  394.8 5.4 %fusion.3 = f32[128,256]{1,0:T(8,128)S(1)} fusion(f32[128,256]{1,0:T(8,128)S(1)} %fusion.12, bf16[16512,128]{1,0:T(8,128)(2,1)S(1)} %collective-permute-done.6, bf16[16512,256]{1,0:T(8,128)(2,1)} %get-tuple-element.83), kind=kOutput, calls=%fused_computation.8 | convolution fusion | flops 1082195968 | bytes 12943360 | tf_op jit(solution)/shard_map/dot_general | solution.py:517
  400.2 1.1 slice-done.1
  401.4 1.5 broadcast_select_fusion.1
  404.2 1.8 collective-permute-start.8
  406.1 1.0 collective-permute-done.8
  407.2 71.8 %collective-permute-start.9 = (f32[32,2048]{1,0:T(8,128)S(1)}, f32[32,2048]{1,0:T(8,128)S(1)}, u32[]{:S(2)}, u32[]{:S(2)}) collective-permute-start(f32[32,2048]{1,0:T(8,128)S(1)} %add.530), channel_id=1, source_target_pairs={{0,64},{2,66},{4,68},{6,70},{8,72},{10,74},{12,76},{14,78},{16,80}... | collective-permute-start | bytes 786440 | tf_op jit(solution)/shard_map/ppermute | solution.py:362
  479.1 6.5 %collective-permute-done.9 = f32[32,2048]{1,0:T(8,128)S(1)} collective-permute-done((f32[32,2048]{1,0:T(8,128)S(1)}, f32[32,2048]{1,0:T(8,128)S(1)}, u32[]{:S(2)}, u32[]{:S(2)}) %collective-permute-start.9) | collective-permute-done | bytes 262176 | tf_op jit(solution)/shard_map/ppermute | solution.py:362
  486.2 1.9 collective-permute-start.10
  488.2 4.2 collective-permute-done.12
  492.5 1.1 collective-permute-done.11
  493.6 1.9 collective-permute-done.10
  495.8 8.0 %collective-permute-start.15 = (f32[4,2048]{1,0:T(4,128)S(1)}, f32[4,2048]{1,0:T(4,128)S(1)}, u32[]{:S(2)}, u32[]{:S(2)}) collective-permute-start(f32[4,2048]{1,0:T(4,128)S(1)} %get-tuple-element.115), channel_id=1, source_target_pairs={{0,48},{2,50},{4,52},{6,54},{8,56},{10,58},{12,60},{14,62},{16,0},... | collective-permute-start | bytes 98312 | tf_op jit(solution)/shard_map/ppermute | solution.py:362
  505.4 3.9 collective-permute-done.14
  (142 shorter events, 18.3 us)
Async XLA Ops:
  0.6 45.6 %copy-start = (s32[8,8]{1,0:T(8,128)S(1)}, s32[8,8]{1,0:T(8,128)}, u32[]{:S(2)}) copy-start(s32[8,8]{1,0:T(8,128)} %param.15) | copy-start | bytes 772
  2.2 36.9 %copy-start.17 = (s32[64,576]{1,0:T(8,128)S(1)}, s32[64,576]{1,0:T(8,128)}, u32[]{:S(2)}) copy-start(s32[64,576]{1,0:T(8,128)} %param.13) | copy-start | bytes 442372
  2.2 38.4 %copy-start.18 = (bf16[64,64]{1,0:T(8,128)(2,1)S(1)}, bf16[64,64]{1,0:T(8,128)(2,1)}, u32[]{:S(2)}) copy-start(bf16[64,64]{1,0:T(8,128)(2,1)} %param.12) | copy-start | bytes 24580
  2.2 39.9 %copy-start.34 = (f32[64,576]{1,0:T(8,128)S(1)}, f32[64,576]{1,0:T(8,128)}, u32[]{:S(2)}) copy-start(f32[64,576]{1,0:T(8,128)} %param.10) | copy-start | bytes 442372
  2.2 47.2 %copy-start.19 = (bf16[64,64]{1,0:T(8,128)(2,1)S(1)}, bf16[64,64]{1,0:T(8,128)(2,1)}, u32[]{:S(2)}) copy-start(bf16[64,64]{1,0:T(8,128)(2,1)} %param.11) | copy-start | bytes 24580
  34.1 3.6 copy-start.10
  37.7 65.8 %collective-permute-start = (bf16[1376,128]{1,0:T(8,128)(2,1)}, bf16[1376,128]{1,0:T(8,128)(2,1)S(1)}, u32[]{:S(2)}, u32[]{:S(2)}) collective-permute-start(bf16[1376,128]{1,0:T(8,128)(2,1)} %get-tuple-element.50), channel_id=1, source_target_pairs={{2,0},{4,2},{6,4},{8,6},{10,8},{12,10},{14,12},{16,14},{18,16},{20... | collective-permute-start | bytes 1056776 | tf_op jit(solution)/shard_map/ppermute | solution.py:40
  47.4 54.2 %copy-start.24 = (pred[32]{0:T(512)(128)(4,1)}, pred[32]{0:T(512)(128)(4,1)S(1)}, u32[]{:S(2)}) copy-start(pred[32]{0:T(512)(128)(4,1)S(1)} %get-tuple-element.120) | copy-start | bytes 100
  47.4 54.8 %copy-start.27 = (pred[32]{0:T(512)(128)(4,1)}, pred[32]{0:T(512)(128)(4,1)S(1)}, u32[]{:S(2)}) copy-start(pred[32]{0:T(512)(128)(4,1)S(1)} %get-tuple-element.123) | copy-start | bytes 100
  50.0 3.6 copy-start.3
  53.6 3.6 copy-start.7
  57.2 3.7 copy-start.11
  98.0 3.6 copy-start.12
  111.5 3.7 copy-start.13
  138.5 40.8 %collective-permute-start.1 = (bf16[1376,128]{1,0:T(8,128)(2,1)}, bf16[1376,128]{1,0:T(8,128)(2,1)S(1)}, u32[]{:S(2)}, u32[]{:S(2)}) collective-permute-start(bf16[1376,128]{1,0:T(8,128)(2,1)} %get-tuple-element.61), channel_id=1, source_target_pairs={{0,2},{2,4},{4,6},{6,8},{8,10},{10,12},{12,14},{14,16},{16,18},{18... | collective-permute-start | bytes 1056776 | tf_op jit(solution)/shard_map/ppermute | solution.py:40
  141.5 37.8 %copy-start.14 = (f32[1376,128]{1,0:T(8,128)S(1)}, f32[1376,128]{1,0:T(8,128)}, u32[]{:S(2)}) copy-start(f32[1376,128]{1,0:T(8,128)} %get-tuple-element.59) | copy-start | bytes 2113540
  141.6 37.8 %copy-start.15 = (f32[1376,128]{1,0:T(8,128)S(1)}, f32[1376,128]{1,0:T(8,128)}, u32[]{:S(2)}) copy-start(f32[1376,128]{1,0:T(8,128)} %get-tuple-element.62) | copy-start | bytes 2113540
  181.4 31.8 %collective-permute-start.2 = (bf16[1376,128]{1,0:T(8,128)(2,1)S(1)}, bf16[1376,128]{1,0:T(8,128)(2,1)S(1)}, u32[]{:S(2)}, u32[]{:S(2)}) collective-permute-start(bf16[1376,128]{1,0:T(8,128)(2,1)S(1)} %get-tuple-element.106), channel_id=1, source_target_pairs={{2,0},{4,2},{6,4},{8,6},{10,8},{12,10},{14,12},{16,14},{18,16},{20... | collective-permute-start | bytes 1056776 | tf_op jit(solution)/shard_map/ppermute | solution.py:40
  237.3 44.0 %collective-permute-start.3 = (bf16[1376,128]{1,0:T(8,128)(2,1)}, bf16[1376,128]{1,0:T(8,128)(2,1)S(1)}, u32[]{:S(2)}, u32[]{:S(2)}) collective-permute-start(bf16[1376,128]{1,0:T(8,128)(2,1)} %get-tuple-element.74), channel_id=1, source_target_pairs={{0,2},{2,4},{4,6},{6,8},{8,10},{10,12},{12,14},{14,16},{16,18},{18... | collective-permute-start | bytes 1056776 | tf_op jit(solution)/shard_map/ppermute | solution.py:40
  241.5 39.9 %copy-start.16 = (f32[1376,128]{1,0:T(8,128)S(1)}, f32[1376,128]{1,0:T(8,128)}, u32[]{:S(2)}) copy-start(f32[1376,128]{1,0:T(8,128)} %get-tuple-element.60) | copy-start | bytes 2113540
  279.7 115.0 %collective-permute-start.6 = (bf16[16512,128]{1,0:T(8,128)(2,1)}, bf16[16512,128]{1,0:T(8,128)(2,1)S(1)}, u32[]{:S(2)}, u32[]{:S(2)}) collective-permute-start(bf16[16512,128]{1,0:T(8,128)(2,1)} %get-tuple-element.81.refs_11_), channel_id=1, source_target_pairs={{0,1},{1,0},{2,3},{3,2},{4,5},{5,4},{6,7},{7,6},{8,9},{9,8},{10,11... | collective-permute-start | bytes 12681224 | tf_op jit(solution)/shard_map/ppermute | solution.py:493
  284.5 109.9 %collective-permute-start.7 = (bf16[1376,128]{1,0:T(8,128)(2,1)S(1)}, bf16[1376,128]{1,0:T(8,128)(2,1)S(1)}, u32[]{:S(2)}, u32[]{:S(2)}) collective-permute-start(bf16[1376,128]{1,0:T(8,128)(2,1)S(1)} %get-tuple-element.102), channel_id=1, source_target_pairs={{0,1},{1,0},{2,3},{3,2},{4,5},{5,4},{6,7},{7,6},{8,9},{9,8},{10,11... | collective-permute-start | bytes 1056776 | tf_op jit(solution)/shard_map/ppermute | solution.py:498
  285.0 31.6 %collective-permute-start.4 = (bf16[1376,128]{1,0:T(8,128)(2,1)S(1)}, bf16[1376,128]{1,0:T(8,128)(2,1)S(1)}, u32[]{:S(2)}, u32[]{:S(2)}) collective-permute-start(bf16[1376,128]{1,0:T(8,128)(2,1)S(1)} %get-tuple-element.104), channel_id=1, source_target_pairs={{2,0},{4,2},{6,4},{8,6},{10,8},{12,10},{14,12},{16,14},{18,16},{20... | collective-permute-start | bytes 1056776 | tf_op jit(solution)/shard_map/ppermute | solution.py:40
  340.8 52.1 %collective-permute-start.5 = (bf16[1376,128]{1,0:T(8,128)(2,1)}, bf16[1376,128]{1,0:T(8,128)(2,1)S(1)}, u32[]{:S(2)}, u32[]{:S(2)}) collective-permute-start(bf16[1376,128]{1,0:T(8,128)(2,1)} %get-tuple-element.85), channel_id=1, source_target_pairs={{0,2},{2,4},{4,6},{6,8},{8,10},{10,12},{12,14},{14,16},{16,18},{18... | collective-permute-start | bytes 1056776 | tf_op jit(solution)/shard_map/ppermute | solution.py:40
  394.1 6.1 %slice-start.3 = ((s8[4227072]{0:T(1024)(128)(4,1)}), s8[4194304]{0:T(1024)(128)(4,1)S(1)}, s32[]{:S(2)}) async-start(s8[4227072]{0:T(1024)(128)(4,1)} %bitcast.33), calls=%async_computation.3 | async-start | bytes 8388608
  394.4 5.7 %slice-start = ((s8[8454144]{0:T(1024)(128)(4,1)}), s8[4194304]{0:T(1024)(128)(4,1)S(1)}, s32[]{:S(2)}) async-start(s8[8454144]{0:T(1024)(128)(4,1)} %bitcast.31), calls=%async_computation | async-start | bytes 8388608
  394.8 6.6 %slice-start.1 = ((s8[8454144]{0:T(1024)(128)(4,1)}), s8[4194304]{0:T(1024)(128)(4,1)S(1)}, s32[]{:S(2)}) async-start(s8[8454144]{0:T(1024)(128)(4,1)} %bitcast.31), calls=%async_computation.1 | async-start | bytes 8388608
  394.8 6.6 %slice-start.2 = ((s8[8454144]{0:T(1024)(128)(4,1)}), s8[65536]{0:T(1024)(128)(4,1)S(1)}, s32[]{:S(2)}) async-start(s8[8454144]{0:T(1024)(128)(4,1)} %bitcast.31), calls=%async_computation.2 | async-start | bytes 131072
  394.8 6.5 %slice-start.4 = ((s8[4227072]{0:T(1024)(128)(4,1)}), s8[32768]{0:T(1024)(128)(4,1)S(1)}, s32[]{:S(2)}) async-start(s8[4227072]{0:T(1024)(128)(4,1)} %bitcast.33), calls=%async_computation.4 | async-start | bytes 65536
  401.3 4.6 copy-start.23
  401.3 4.7 copy-start.25
  401.3 4.7 copy-start.28
  401.4 4.7 copy-start.29
  401.4 4.7 copy-start.30
  401.4 77.6 %copy-start.26 = (pred[32]{0:T(512)(128)(4,1)S(1)}, pred[32]{0:T(512)(128)(4,1)}, u32[]{:S(2)}) copy-start(pred[32]{0:T(512)(128)(4,1)} %get-tuple-element.94) | copy-start | bytes 100
  401.4 84.2 %copy-start.20 = (pred[16,32]{1,0:T(8,128)(4,1)S(1)}, pred[16,32]{1,0:T(8,128)(4,1)}, u32[]{:S(2)}) copy-start(pred[16,32]{1,0:T(8,128)(4,1)} %fusion.46) | copy-start | bytes 1540
  401.4 84.2 %copy-start.21 = (pred[16,32]{1,0:T(8,128)(4,1)S(1)}, pred[16,32]{1,0:T(8,128)(4,1)}, u32[]{:S(2)}) copy-start(pred[16,32]{1,0:T(8,128)(4,1)} %fusion.45) | copy-start | bytes 1540
  401.4 86.7 %copy-start.35 = (pred[1,4,32]{2,1,0:T(4,128)(4,1)S(1)}, pred[1,4,32]{2,1,0:T(4,128)(4,1)}, u32[]{:S(2)}) copy-start(pred[1,4,32]{2,1,0:T(4,128)(4,1)} %fusion.64) | copy-start | bytes 388
  401.4 86.7 %copy-start.36 = (pred[1,4,32]{2,1,0:T(4,128)(4,1)S(1)}, pred[1,4,32]{2,1,0:T(4,128)(4,1)}, u32[]{:S(2)}) copy-start(pred[1,4,32]{2,1,0:T(4,128)(4,1)} %fusion.63) | copy-start | bytes 388
  401.4 108.5 %copy-start.1 = (s32[8,8]{1,0:T(8,128)S(1)}, s32[8,8]{1,0:T(8,128)}, u32[]{:S(2)}) copy-start(s32[8,8]{1,0:T(8,128)} %param.15) | copy-start | bytes 772
  404.2 3.0 collective-permute-start.8
  407.2 78.4 %collective-permute-start.9 = (f32[32,2048]{1,0:T(8,128)S(1)}, f32[32,2048]{1,0:T(8,128)S(1)}, u32[]{:S(2)}, u32[]{:S(2)}) collective-permute-start(f32[32,2048]{1,0:T(8,128)S(1)} %add.530), channel_id=1, source_target_pairs={{0,64},{2,66},{4,68},{6,70},{8,72},{10,74},{12,76},{14,78},{16,80}... | collective-permute-start | bytes 786440 | tf_op jit(solution)/shard_map/ppermute | solution.py:362
  486.0 6.5 %collective-permute-start.12 = (f32[16,2048]{1,0:T(8,128)S(1)}, f32[16,2048]{1,0:T(8,128)S(1)}, u32[]{:S(2)}, u32[]{:S(2)}) collective-permute-start(f32[16,2048]{1,0:T(8,128)S(1)} %get-tuple-element.108), channel_id=1, source_target_pairs={{0,12},{2,14},{4,0},{6,2},{8,4},{10,6},{12,8},{14,10},{16,28},{18,... | collective-permute-start | bytes 393224 | tf_op jit(solution)/shard_map/ppermute | solution.py:362
  486.1 7.5 %collective-permute-start.11 = (f32[16,2048]{1,0:T(8,128)S(1)}, f32[16,2048]{1,0:T(8,128)S(1)}, u32[]{:S(2)}, u32[]{:S(2)}) collective-permute-start(f32[16,2048]{1,0:T(8,128)S(1)} %get-tuple-element.109), channel_id=1, source_target_pairs={{0,8},{2,10},{4,12},{6,14},{8,0},{10,2},{12,4},{14,6},{16,24},{18,... | collective-permute-start | bytes 393224 | tf_op jit(solution)/shard_map/ppermute | solution.py:362
  486.2 9.3 %collective-permute-start.10 = (f32[16,2048]{1,0:T(8,128)S(1)}, f32[16,2048]{1,0:T(8,128)S(1)}, u32[]{:S(2)}, u32[]{:S(2)}) collective-permute-start(f32[16,2048]{1,0:T(8,128)S(1)} %get-tuple-element.107), channel_id=1, source_target_pairs={{0,4},{2,6},{4,8},{6,10},{8,12},{10,14},{12,0},{14,2},{16,20},{18,... | collective-permute-start | bytes 393224 | tf_op jit(solution)/shard_map/ppermute | solution.py:362
  495.8 9.6 %collective-permute-start.15 = (f32[4,2048]{1,0:T(4,128)S(1)}, f32[4,2048]{1,0:T(4,128)S(1)}, u32[]{:S(2)}, u32[]{:S(2)}) collective-permute-start(f32[4,2048]{1,0:T(4,128)S(1)} %get-tuple-element.115), channel_id=1, source_target_pairs={{0,48},{2,50},{4,52},{6,54},{8,56},{10,58},{12,60},{14,62},{16,0},... | collective-permute-start | bytes 98312 | tf_op jit(solution)/shard_map/ppermute | solution.py:362
  503.8 5.5 %collective-permute-start.14 = (f32[4,2048]{1,0:T(4,128)S(1)}, f32[4,2048]{1,0:T(4,128)S(1)}, u32[]{:S(2)}, u32[]{:S(2)}) collective-permute-start(f32[4,2048]{1,0:T(4,128)S(1)} %get-tuple-element.116), channel_id=1, source_target_pairs={{0,32},{2,34},{4,36},{6,38},{8,40},{10,42},{12,44},{14,46},{16,48}... | collective-permute-start | bytes 98312 | tf_op jit(solution)/shard_map/ppermute | solution.py:362
  503.8 5.5 %collective-permute-start.13 = (f32[4,2048]{1,0:T(4,128)S(1)}, f32[4,2048]{1,0:T(4,128)S(1)}, u32[]{:S(2)}, u32[]{:S(2)}) collective-permute-start(f32[4,2048]{1,0:T(4,128)S(1)} %get-tuple-element.114), channel_id=1, source_target_pairs={{0,16},{2,18},{4,20},{6,22},{8,24},{10,26},{12,28},{14,30},{16,32}... | collective-permute-start | bytes 98312 | tf_op jit(solution)/shard_map/ppermute | solution.py:362
  (10 other events, 24.3 us)
